TPU v7x, 32 devices: a whole 2x2x4 slice. The times are simulated.
32 devices in a mesh: rows: 8 (over z, y), heads: 4 (over x, core).
Axes of the slice: x: 2, y: 2, z: 4, core: 2. Of those that a mesh axis runs over, the one named last changes fastest.
Arguments:
- tokens: bfloat16 [32768, 768], P('rows')
- cotangent: bfloat16 [32768, 768], P(('rows', 'heads')), may hold values from -6 to 6
- bucket: int32 [64], P('rows'), may hold values from 0 to 2, as said below
- lengths: int32 [64, 8], P('rows'), may hold values from 0 to 512, as said below
- in_weight: float32 [3, 768, 768], P(None, 'rows', 'heads'), may hold values from -0.21875 to 0.21875
- in_first: float32 [3, 768, 768], P(None, 'rows', 'heads'), may hold values from -0.00061035156 to 0.00061035156
- in_second: float32 [3, 768, 768], P(None, 'rows', 'heads'), may hold values from 1e-09 to 4e-09
- in_average: float32 [3, 768, 768], P(None, 'rows', 'heads'), may hold values from -0.21875 to 0.21875
- in_bias: float32 [2, 12, 64], P(None, 'heads', 'rows'), may hold values from -1.75 to 1.75
- bias_first: float32 [2, 12, 64], P(None, 'heads', 'rows'), may hold values from -0.0017089844 to 0.0017089844
- bias_second: float32 [2, 12, 64], P(None, 'heads', 'rows'), may hold values from 1e-08 to 4e-08
- bias_average: float32 [2, 12, 64], P(None, 'heads', 'rows'), may hold values from -1.75 to 1.75
- out_weight: float32 [768, 768], P(('rows', 'heads')), may hold values from -0.875 to 0.875
- out_first: float32 [768, 768], P(('rows', 'heads')), may hold values from -0.00061035156 to 0.00061035156
- out_second: float32 [768, 768], P(('rows', 'heads')), may hold values from 1e-09 to 4e-09
- out_average: float32 [768, 768], P(('rows', 'heads')), may hold values from -0.875 to 0.875
- up_weight: float32 [768, 3072], P(('rows', 'heads')), may hold values from -0.21875 to 0.21875
- up_first: float32 [768, 3072], P(('rows', 'heads')), may hold values from -0.00061035156 to 0.00061035156
- up_second: float32 [768, 3072], P(('rows', 'heads')), may hold values from 1e-09 to 4e-09
- up_average: float32 [768, 3072], P(('rows', 'heads')), may hold values from -0.21875 to 0.21875
- down_weight: float32 [3072, 768], P(('rows', 'heads')), may hold values from -0.109375 to 0.109375
- down_first: float32 [3072, 768], P(('rows', 'heads')), may hold values from -0.00061035156 to 0.00061035156
- down_second: float32 [3072, 768], P(('rows', 'heads')), may hold values from 1e-09 to 4e-09
- down_average: float32 [3072, 768], P(('rows', 'heads')), may hold values from -0.109375 to 0.109375
- vectors: float32 [7680], P(('rows', 'heads'))
- vec_first: float32 [7680], P(('rows', 'heads')), may hold values from -0.0017089844 to 0.0017089844
- vec_second: float32 [7680], P(('rows', 'heads')), may hold values from 1e-08 to 4e-08
- vec_average: float32 [7680], P(('rows', 'heads'))
Outputs:
- layer_out: bfloat16 [32768, 768], P(('rows', 'heads'))
- token_grad: float32 [32768, 768], P(('rows', 'heads'))
- grad_norm: float32 [], replicated
- in_weight_new: float32 [3, 768, 768], P(None, 'rows', 'heads')
- in_first_new: float32 [3, 768, 768], P(None, 'rows', 'heads')
- in_second_new: float32 [3, 768, 768], P(None, 'rows', 'heads')
- in_average_new: float32 [3, 768, 768], P(None, 'rows', 'heads')
- in_bias_new: float32 [2, 12, 64], P(None, 'heads', 'rows')
- bias_first_new: float32 [2, 12, 64], P(None, 'heads', 'rows')
- bias_second_new: float32 [2, 12, 64], P(None, 'heads', 'rows')
- bias_average_new: float32 [2, 12, 64], P(None, 'heads', 'rows')
- out_weight_new: float32 [768, 768], P(('rows', 'heads'))
- out_first_new: float32 [768, 768], P(('rows', 'heads'))
- out_second_new: float32 [768, 768], P(('rows', 'heads'))
- out_average_new: float32 [768, 768], P(('rows', 'heads'))
- up_weight_new: float32 [768, 3072], P(('rows', 'heads'))
- up_first_new: float32 [768, 3072], P(('rows', 'heads'))
- up_second_new: float32 [768, 3072], P(('rows', 'heads'))
- up_average_new: float32 [768, 3072], P(('rows', 'heads'))
- down_weight_new: float32 [3072, 768], P(('rows', 'heads'))
- down_first_new: float32 [3072, 768], P(('rows', 'heads'))
- down_second_new: float32 [3072, 768], P(('rows', 'heads'))
- down_average_new: float32 [3072, 768], P(('rows', 'heads'))
- vectors_new: float32 [7680], P(('rows', 'heads'))
- vec_first_new: float32 [7680], P(('rows', 'heads'))
- vec_second_new: float32 [7680], P(('rows', 'heads'))
- vec_average_new: float32 [7680], P(('rows', 'heads'))
Inputs may be any that keep to these rules, and one draw needn't show every extreme that they name: Block b of 512 slots holds one slot row of 512 slots when bucket[b] is 0, rows of 128 slots filling it when 1, rows of 64 slots filling it when 2. Among the 8 blocks of each index of rows there is at least one of kind 0. lengths[b, r] is the number of live tokens at the start of slot row r of block b, 1 to that row's capacity for the rows that the block's kind has, and 0 for the entries beyond them. Among the blocks of each index of rows, one of kind 0 has its row full.
All inputs are finite; a program needn't handle non-finite values.
Results may differ from a plain program's by a relative error of at most 0.013.
The roundings to bfloat16 on the way count: a program that leaves them out, or rounds other values in their place, can miss the bound.
Values may be sent and summed in bfloat16 or wider, within the bound.
No kernel may reach another device: no remote copies, remote signals or barrier semaphores. Data moves between devices by JAX's collectives and lax.ppermute only.
A program may use at most 192 MiB of HBM per device.

v0:
```python
from functools import partial
import math

import jax
import jax.numpy as jnp
from jax import lax
from jax.sharding import PartitionSpec as P

D = 768
HD = 64
FF = 3072
CAP_L = 512
CAP_M = 128
CAP_S = 64
BLK_DEV = 8
STEP = 10
ROWS_BLK = 8
PARAMS = 7087104


LN_EPS = 1e-05
LEARN_RATE = 0.1
VECTOR_RATE = 0.3
BETA_ONE = 0.9
BETA_TWO = 0.999
ADAM_EPS = 1e-08
WEIGHT_DECAY = 0.01
AVERAGE_KEEP = 0.75
CLIP_RMS = 0.001


def layer_norm(values, scale_gain, shift_add):
    center = values - jnp.mean(values, axis=-1, keepdims=True)
    spread = jnp.mean(center * center, axis=-1, keepdims=True)
    return center * lax.rsqrt(spread + LN_EPS) * scale_gain + shift_add


def block_mask(block_kind, row_lengths):
    capacity = jnp.where(block_kind == 0, CAP_L, jnp.where(block_kind == 1, CAP_M, CAP_S)).astype(
        jnp.int32
    )
    position = jnp.arange(CAP_L, dtype=jnp.int32)
    row_index = position // capacity
    within = position - row_index * capacity
    slot_index = jnp.arange(ROWS_BLK, dtype=jnp.int32)
    live_length = jnp.sum(
        jnp.where(row_index[:, None] == slot_index[None, :], row_lengths[None, :], 0), axis=1
    )
    is_valid = within < live_length
    return (row_index[:, None] == row_index[None, :]) & is_valid[None, :]


def split_vector(vec_values):
    split_points = [D, D + FF, 2 * D + FF, 3 * D + FF, 4 * D + FF, 5 * D + FF]
    return jnp.split(vec_values, split_points)


def contract_rows(left, right):
    return lax.dot_general(
        left, right, (((0,), (0,)), ((), ())), preferred_element_type=jnp.float32
    )


def contract_cols(left, right):
    return lax.dot_general(
        left, right, (((1,), (1,)), ((), ())), preferred_element_type=jnp.float32
    )


def block_scores(queries, key_rows, key_masks):
    scores = jnp.einsum(
        "qhd,khd->hqk", queries, key_rows, preferred_element_type=jnp.float32
    ) * HD ** (-0.5)
    return jnp.where(key_masks[None], scores, -1e30)


def attend_block(queries, key_rows, values, key_masks):
    scores = block_scores(queries, key_rows, key_masks)
    row_peak = jnp.max(scores, axis=-1, keepdims=True)
    exponent = jnp.exp(scores - row_peak)
    row_total = jnp.sum(exponent, axis=-1, keepdims=True)
    attention = exponent / row_total
    head_out = jnp.einsum(
        "hqk,khd->qhd", attention.astype(jnp.bfloat16), values, preferred_element_type=jnp.float32
    )
    return (head_out.astype(jnp.bfloat16), row_peak + jnp.log(row_total))


def attend_back(queries, key_rows, values, key_masks, row_lse, grad_out):
    scores = block_scores(queries, key_rows, key_masks)
    attention = jnp.exp(scores - row_lse)
    grad_values = jnp.einsum(
        "hqk,qhd->khd", attention.astype(jnp.bfloat16), grad_out, preferred_element_type=jnp.float32
    )
    grad_attention = jnp.einsum(
        "qhd,khd->hqk", grad_out, values, preferred_element_type=jnp.float32
    )
    row_inner = jnp.sum(grad_attention * attention, axis=-1, keepdims=True)
    grad_scores = (attention * (grad_attention - row_inner)).astype(jnp.bfloat16)
    grad_queries = jnp.einsum(
        "hqk,khd->qhd", grad_scores, key_rows, preferred_element_type=jnp.float32
    ) * HD ** (-0.5)
    grad_keys = jnp.einsum(
        "hqk,qhd->khd", grad_scores, queries, preferred_element_type=jnp.float32
    ) * HD ** (-0.5)
    return (
        grad_queries.astype(jnp.bfloat16),
        grad_keys.astype(jnp.bfloat16),
        grad_values.astype(jnp.bfloat16),
    )


def adam_update(weight, first, second, average, gradient, rate):
    first_new = BETA_ONE * first + (1.0 - BETA_ONE) * gradient
    second_new = BETA_TWO * second + (1.0 - BETA_TWO) * gradient * gradient
    first_hat = first_new / (1.0 - BETA_ONE**STEP)
    second_hat = second_new / (1.0 - BETA_TWO**STEP)
    weight_new = weight - rate * (
        first_hat / (jnp.sqrt(second_hat) + ADAM_EPS) + WEIGHT_DECAY * weight
    )
    average_new = AVERAGE_KEEP * average + (1.0 - AVERAGE_KEEP) * weight_new
    return (weight_new, first_new, second_new, average_new)


def body(
    tokens,
    cotangent,
    bucket,
    lengths,
    in_weight,
    in_first,
    in_second,
    in_average,
    in_bias,
    bias_first,
    bias_second,
    bias_average,
    out_weight,
    out_first,
    out_second,
    out_average,
    up_weight,
    up_first,
    up_second,
    up_average,
    down_weight,
    down_first,
    down_second,
    down_average,
    vectors,
    vec_first,
    vec_second,
    vec_average,
):
    head_count = lax.axis_size("heads")
    slot_count = tokens.shape[0]
    token_share = slot_count // head_count
    local_cols = in_weight.shape[2]
    local_heads = local_cols // HD
    gathered_in, gathered_bias = (
        lax.all_gather(in_weight.astype(jnp.bfloat16), "rows", axis=1, tiled=True),
        lax.all_gather(in_bias.astype(jnp.bfloat16), "rows", axis=2, tiled=True),
    )
    gathered_out, gathered_up, gathered_down, gathered_vec = (
        lax.all_gather(out_weight.astype(jnp.bfloat16), ("rows", "heads"), axis=0, tiled=True),
        lax.all_gather(up_weight.astype(jnp.bfloat16), ("rows", "heads"), axis=0, tiled=True),
        lax.all_gather(down_weight.astype(jnp.bfloat16), ("rows", "heads"), axis=0, tiled=True),
        lax.all_gather(vectors.astype(jnp.bfloat16), ("rows", "heads"), axis=0, tiled=True),
    )
    bias_out, bias_up, bias_down, gain_one, shift_one, gain_two, shift_two = split_vector(
        gathered_vec.astype(jnp.float32)
    )
    bias_cols = gathered_bias.astype(jnp.float32).reshape(2, local_cols)
    projected = jnp.einsum("td,jdc->jtc", tokens, gathered_in, preferred_element_type=jnp.float32)
    bias_rows = jnp.stack([bias_cols[0], jnp.zeros_like(bias_cols[0]), bias_cols[1]])
    projected = (projected + bias_rows[:, None, :]).astype(jnp.bfloat16)
    block_view = projected.reshape(3, BLK_DEV, CAP_L, local_heads, HD)
    key_masks = jax.vmap(block_mask)(bucket, lengths)
    head_blocks, block_lse = lax.map(
        lambda block_items: attend_block(*block_items),
        (block_view[0], block_view[1], block_view[2], key_masks),
    )
    head_rows = head_blocks.reshape(slot_count, local_cols)
    token_rows = lax.all_to_all(head_rows, "heads", split_axis=0, concat_axis=1, tiled=True)
    local_inputs = lax.dynamic_slice_in_dim(
        tokens, lax.axis_index("heads") * token_share, token_share, 0
    ).astype(jnp.float32)
    branch = jnp.dot(token_rows, gathered_out, preferred_element_type=jnp.float32) + bias_out
    first_out, first_pull = jax.vjp(layer_norm, local_inputs + branch, gain_one, shift_one)
    first_low = first_out.astype(jnp.bfloat16)
    hidden_pre = jnp.dot(first_low, gathered_up, preferred_element_type=jnp.float32) + bias_up
    hidden_act, gelu_pull = jax.vjp(partial(jax.nn.gelu, approximate=False), hidden_pre)
    hidden_low = hidden_act.astype(jnp.bfloat16)
    ffn_out = jnp.dot(hidden_low, gathered_down, preferred_element_type=jnp.float32) + bias_down
    final_out, final_pull = jax.vjp(layer_norm, first_out + ffn_out, gain_two, shift_two)
    layer_out = final_out.astype(jnp.bfloat16)
    back_in, back_out, back_up, back_down = (gathered_in, gathered_out, gathered_up, gathered_down)
    grad_resid_two, grad_gain_two, grad_shift_two = final_pull(cotangent.astype(jnp.float32))
    grad_ffn = grad_resid_two.astype(jnp.bfloat16)
    grad_down = contract_rows(hidden_low, grad_ffn)
    grad_bias_down = jnp.sum(grad_ffn, axis=0, dtype=jnp.float32)
    (grad_hidden_pre,) = gelu_pull(contract_cols(grad_ffn, back_down))
    grad_pre_low = grad_hidden_pre.astype(jnp.bfloat16)
    grad_up = contract_rows(first_low, grad_pre_low)
    grad_bias_up = jnp.sum(grad_pre_low, axis=0, dtype=jnp.float32)
    grad_first = grad_resid_two + contract_cols(grad_pre_low, back_up)
    grad_resid_one, grad_gain_one, grad_shift_one = first_pull(grad_first)
    grad_branch = grad_resid_one.astype(jnp.bfloat16)
    grad_out = contract_rows(token_rows, grad_branch)
    grad_bias_out = jnp.sum(grad_branch, axis=0, dtype=jnp.float32)
    grad_mixed = contract_cols(grad_branch, back_out).astype(jnp.bfloat16)
    grad_heads = lax.all_to_all(grad_mixed, "heads", split_axis=1, concat_axis=0, tiled=True)
    grad_view = grad_heads.reshape(BLK_DEV, CAP_L, local_heads, HD)
    grads_query, grads_key, grads_value = lax.map(
        lambda block_items: attend_back(*block_items),
        (block_view[0], block_view[1], block_view[2], key_masks, block_lse, grad_view),
    )
    grad_proj = jnp.stack([grads_query, grads_key, grads_value]).reshape(3, slot_count, local_cols)
    grad_in = jnp.einsum("td,jtc->jdc", tokens, grad_proj, preferred_element_type=jnp.float32)
    grad_bias = jnp.stack(
        [
            jnp.sum(grad_proj[0], axis=0, dtype=jnp.float32),
            jnp.sum(grad_proj[2], axis=0, dtype=jnp.float32),
        ]
    ).reshape(2, local_heads, HD)
    owner_proj = lax.all_to_all(grad_proj, "heads", split_axis=1, concat_axis=2, tiled=True)
    whole_in = lax.all_gather(back_in, "heads", axis=2, tiled=True)
    token_grad = (
        jnp.einsum("jtc,jdc->td", owner_proj, whole_in, preferred_element_type=jnp.float32)
        + grad_resid_one
    )
    sum_in, sum_bias = (
        lax.psum_scatter(grad_in, "rows", scatter_dimension=1, tiled=True),
        lax.psum_scatter(grad_bias, "rows", scatter_dimension=2, tiled=True),
    )
    grad_vec = jnp.concatenate(
        [
            grad_bias_out,
            grad_bias_up,
            grad_bias_down,
            grad_gain_one,
            grad_shift_one,
            grad_gain_two,
            grad_shift_two,
        ]
    )
    sum_out, sum_up, sum_down, sum_vec = (
        lax.psum_scatter(grad_out, ("rows", "heads"), scatter_dimension=0, tiled=True),
        lax.psum_scatter(grad_up, ("rows", "heads"), scatter_dimension=0, tiled=True),
        lax.psum_scatter(grad_down, ("rows", "heads"), scatter_dimension=0, tiled=True),
        lax.psum_scatter(grad_vec, ("rows", "heads"), scatter_dimension=0, tiled=True),
    )
    local_square = (
        jnp.sum(sum_in * sum_in)
        + jnp.sum(sum_bias * sum_bias)
        + jnp.sum(sum_out * sum_out)
        + jnp.sum(sum_up * sum_up)
        + jnp.sum(sum_down * sum_down)
        + jnp.sum(sum_vec * sum_vec)
    )
    grad_norm = jnp.sqrt(lax.psum(local_square, ("rows", "heads")))
    clip_limit = CLIP_RMS * math.sqrt(PARAMS)
    factor = clip_limit / jnp.maximum(grad_norm, clip_limit)
    in_new = adam_update(in_weight, in_first, in_second, in_average, sum_in * factor, LEARN_RATE)
    bias_new = adam_update(
        in_bias, bias_first, bias_second, bias_average, sum_bias * factor, LEARN_RATE
    )
    out_new = adam_update(
        out_weight, out_first, out_second, out_average, sum_out * factor, LEARN_RATE
    )
    up_new = adam_update(up_weight, up_first, up_second, up_average, sum_up * factor, LEARN_RATE)
    down_new = adam_update(
        down_weight, down_first, down_second, down_average, sum_down * factor, LEARN_RATE
    )
    vec_new = adam_update(
        vectors, vec_first, vec_second, vec_average, sum_vec * factor, VECTOR_RATE
    )
    return (
        layer_out,
        token_grad,
        grad_norm,
        in_new[0],
        in_new[1],
        in_new[2],
        in_new[3],
        bias_new[0],
        bias_new[1],
        bias_new[2],
        bias_new[3],
        out_new[0],
        out_new[1],
        out_new[2],
        out_new[3],
        up_new[0],
        up_new[1],
        up_new[2],
        up_new[3],
        down_new[0],
        down_new[1],
        down_new[2],
        down_new[3],
        vec_new[0],
        vec_new[1],
        vec_new[2],
        vec_new[3],
    )


def solution(mesh):
    in_specs = (
        P("rows", None),
        P(("rows", "heads"), None),
        P("rows"),
        P("rows", None),
        P(None, "rows", "heads"),
        P(None, "rows", "heads"),
        P(None, "rows", "heads"),
        P(None, "rows", "heads"),
        P(None, "heads", "rows"),
        P(None, "heads", "rows"),
        P(None, "heads", "rows"),
        P(None, "heads", "rows"),
        P(("rows", "heads"), None),
        P(("rows", "heads"), None),
        P(("rows", "heads"), None),
        P(("rows", "heads"), None),
        P(("rows", "heads"), None),
        P(("rows", "heads"), None),
        P(("rows", "heads"), None),
        P(("rows", "heads"), None),
        P(("rows", "heads"), None),
        P(("rows", "heads"), None),
        P(("rows", "heads"), None),
        P(("rows", "heads"), None),
        P(("rows", "heads")),
        P(("rows", "heads")),
        P(("rows", "heads")),
        P(("rows", "heads")),
    )
    out_specs = (
        P(("rows", "heads"), None),
        P(("rows", "heads"), None),
        P(),
        P(None, "rows", "heads"),
        P(None, "rows", "heads"),
        P(None, "rows", "heads"),
        P(None, "rows", "heads"),
        P(None, "heads", "rows"),
        P(None, "heads", "rows"),
        P(None, "heads", "rows"),
        P(None, "heads", "rows"),
        P(("rows", "heads"), None),
        P(("rows", "heads"), None),
        P(("rows", "heads"), None),
        P(("rows", "heads"), None),
        P(("rows", "heads"), None),
        P(("rows", "heads"), None),
        P(("rows", "heads"), None),
        P(("rows", "heads"), None),
        P(("rows", "heads"), None),
        P(("rows", "heads"), None),
        P(("rows", "heads"), None),
        P(("rows", "heads"), None),
        P(("rows", "heads")),
        P(("rows", "heads")),
        P(("rows", "heads")),
        P(("rows", "heads")),
    )
    return jax.shard_map(body, mesh=mesh, in_specs=in_specs, out_specs=out_specs, check_vma=False)
```

profile of v0, /device:TPU:0, one launch (start us, length us, event | category | flops | bytes accessed | tf_op | source)
XLA Modules:
  0.0 897.6 jit_solution(17077085537927906205)
XLA Ops:
  16.0 32.2 %all_gather.22 = bf16[2,3,64]{1,0,2:T(2,128)(2,1)S(1)} all-gather(bf16[2,3,8]{1,0,2:T(2,128)(2,1)S(1)} %copy.287), channel_id=1, replica_groups=mesh['rows'=8,'heads'=4] {'rows'}, dimensions={2}, use_global_device_ids=true | all-gather | bytes 864 | tf_op jit(solution)/shard_map/all_gather | solution.py:162
  48.7 41.0 %all_gather.21 = bf16[3,768,192]{2,0,1:T(4,128)(2,1)} all-gather(bf16[3,96,192]{2,0,1:T(4,128)(2,1)S(1)} %copy.285), channel_id=1, replica_groups=mesh['rows'=8,'heads'=4] {'rows'}, dimensions={1}, use_global_device_ids=true | all-gather | bytes 995328 | tf_op jit(solution)/shard_map/all_gather | solution.py:161
  89.8 2.6 copy.286
  92.5 7.1 fusion.66
  108.1 46.8 %while.26 = (s32[]{:T(128)}, bf16[8,512,3,64]{1,3,2,0:T(8,128)(2,1)}, f32[8,3,512,1]{2,1,3,0:T(4,128)}, bf16[8,512,3,64]{1,3,2,0:T(8,128)(2,1)}, pred[8,512,512]...) while((s32[]{:T(128)}, ...), condition=%wide.region_4.5_spmd, body=%wide.region_1.4_spmd.sunk | while | flops 210860544 | bytes 11588185 | solution.py:179
  111.3 2.7 fusion.152
  117.1 2.7 fusion.152
  119.8 2.0 fusion.150
  123.1 2.7 fusion.152
  128.9 2.7 fusion.152
  134.8 2.7 fusion.152
  140.6 2.7 fusion.152
  146.4 2.7 fusion.152
  152.3 2.7 fusion.152
  154.9 4.2 copy.293
  159.1 3.7 all_to_all.39
  162.8 3.1 copy.294
  165.9 4.4 all-to-all-start
  174.6 48.7 %all-reduce = bf16[7680]{0:T(1024)(128)(2,1)S(1)} all-reduce(bf16[7680]{0:T(1024)(128)(2,1)S(1)} %dynamic-update-slice), channel_id=1, replica_groups=mesh['rows'=8,'heads'=4] {'rows','heads'}, use_global_device_ids=true, to_apply=%add | all-reduce | flops 7680 | bytes 30720
  224.1 3.9 fusion.108
  230.2 37.8 %multiply_convert_fusion.1 = (bf16[1024,3072]{1,0:T(8,128)(2,1)}, f32[1024,3072]{1,0:T(8,128)}, f32[1024,3072]{1,0:T(8,128)}) fusion(f32[3072]{0:T(1024)S(1)} %split.31, bf16[768,3072]{1,0:T(8,128)(2,1)} %all-gather.7.cloned.1.call-done, f32[1024,768]{0,1:T(8,128)} %copy-done.2, f32[768]{0:T(1024)S(1)} %get-tuple-element.478, ...), kind=kOutput, calls=%fused_computation.64 | convolution fusion | flops 5043388416 | bytes 39348224 | tf_op jit(solution)/shard_map/dot_general | solution.py:191
  267.9 9.8 %fusion.109 = (f32[1024]{0:T(1024)S(1)}, f32[1024,768]{0,1:T(8,128)S(1)}) fusion(f32[768]{0:T(1024)S(1)} %get-tuple-element.476, bf16[1024,3072]{1,0:T(8,128)(2,1)} %get-tuple-element.460, bf16[3072,768]{1,0:T(8,128)(2,1)} %all-gather.9.cloned.1.call-done, f32[768]{0:T(1024)S(1)} %get-tuple-element.478, f32[768]{0:T(1024)S(1)} %get-tuple-element.477, ...), kind=kOutput, calls=%fused_computation.196 | convolution fusion | flops 4837342208 | bytes 17323008 | tf_op jit(solution)/shard_map/dot_general | solution.py:194
  280.5 2.7 convert_reduce_fusion.2
  283.3 17.6 %convert_reduce_fusion = (f32[3072]{0:T(1024)S(1)}, bf16[1024,3072]{1,0:T(8,128)(2,1)}) fusion(f32[1024,3072]{1,0:T(8,128)} %get-tuple-element.461, bf16[1024,768]{0,1:T(8,128)(2,1)S(1)} %get-tuple-element.455, bf16[3072,768]{1,0:T(8,128)(2,1)} %all-gather.9.cloned.1.call-done, f32[1024,3072]{1,0:T(8,128)} %get-tuple-element.484, f32[3072]{0:T(1024)S(1)} %split.31), kind=kOutput, calls=%fused_computation.62 | convolution fusion | flops 4885312512 | bytes 37773312 | tf_op jit(solution)/shard_map/dot_general | solution.py:65
  300.8 10.9 %multiply_reduce_fusion.1 = (f32[768]{0:T(1024)S(1)}, f32[1024]{0:T(1024)S(1)}, f32[768]{0:T(1024)S(1)}, f32[1024,768]{0,1:T(8,128)S(1)}) fusion(f32[1024,768]{0,1:T(8,128)} %copy-done.2, f32[1024]{0:T(1024)S(1)} %fusion.87, f32[1024]{0:T(1024)S(1)} %broadcast_multiply_fusion.1, f32[768]{0:T(1024)S(1)} %get-tuple-element.477, ...), kind=kOutput, calls=%fused_computation.95 | convolution fusion | flops 4845204480 | bytes 22061056 | tf_op jit(solution)/shard_map/dot_general | solution.py:65
  314.8 2.5 convolution_convert_fusion
  317.3 3.6 all-to-all-start.1
  320.9 4.3 fusion.110
  325.3 15.7 %all-to-all-done.1 = bf16[1024,4,192]{0,2,1:T(8,128)(2,1)S(1)} async-done(((bf16[1024,4,192]{0,2,1:T(8,128)(2,1)}), bf16[1024,4,192]{0,2,1:T(8,128)(2,1)S(1)}, u32[]{:S(2)}, u32[]{:S(2)}) %all-to-all-start.1) | async-done | bytes 1572896 | tf_op jit(solution)/shard_map/all_to_all | solution.py:212
  346.1 90.0 %while.27 = (s32[]{:T(128)}, bf16[8,512,3,64]{1,3,2,0:T(8,128)(2,1)S(1)}, bf16[8,512,3,64]{1,3,2,0:T(8,128)(2,1)}, bf16[8,512,3,64]{1,3,2,0:T(8,128)(2,1)S(1)}, ...) while((s32[]{:T(128)}, ...), condition=%wide.region_15.16_spmd, body=%wide.region_13.15_spmd.sunk | while | flops 510884352 | bytes 26381428 | solution.py:214
  347.8 2.0 subtract_exponential_fusion.3
  352.3 2.2 fusion.162
  359.1 2.0 subtract_exponential_fusion.3
  363.6 2.2 fusion.162
  374.8 2.2 fusion.162
  386.1 2.2 fusion.162
  397.3 2.2 fusion.162
  404.0 2.0 subtract_exponential_fusion.3
  408.5 2.2 fusion.162
  419.8 2.2 fusion.162
  431.0 2.2 fusion.162
  436.1 2.0 copy.302
  438.1 3.8 stack.25
  441.8 3.4 copy.303
  445.2 3.7 stack.26
  449.0 2.0 copy.304
  451.0 3.7 stack.27
  457.2 2.1 copy-done.5
  459.4 7.1 fusion.74
  466.5 4.2 copy.341
  470.7 4.7 reshape.394
  476.1 10.9 %fusion.90 = f32[768,3072]{1,0:T(8,128)} fusion(bf16[1024,3072]{1,0:T(8,128)(2,1)} %get-tuple-element.489, f32[1024,768]{0,1:T(8,128)} %copy-done.2, f32[768]{0:T(1024)S(1)} %get-tuple-element.478, f32[768]{0:T(1024)S(1)} %get-tuple-element.477, f32[1024]{0:T(1024)S(1)} %fusion.87, f32[1024]{0:T(1024)S(1)} %broadcast_multiply_fusion.1), kind=kOutput, calls=%fused_computation.187 | convolution fusion | flops 4835770368 | bytes 18888704 | tf_op jit(solution)/shard_map/dot_general | solution.py:59
  487.0 9.9 %fusion.111 = f32[3072,768]{1,0:T(8,128)} fusion(bf16[1024,3072]{1,0:T(8,128)(2,1)} %get-tuple-element.460, bf16[1024,768]{0,1:T(8,128)(2,1)} %copy-done.10), kind=kOutput, calls=%fused_computation.198 | convolution fusion | flops 4831838208 | bytes 17301504 | tf_op jit(solution)/shard_map/dot_general | solution.py:59
  496.9 12.8 %copy.305 = bf16[3,4096,192]{2,0,1:T(4,128)(2,1)} copy(bf16[3,4096,192]{1,2,0:T(8,128)(2,1)} %copy-done.5) | data formatting | bytes 9437184 | tf_op jit(solution)/shard_map/stack | solution.py:218
  509.7 5.8 all-to-all-start.2
  523.1 2.6 copy.321
  525.8 124.5 %all-reduce.2 = f32[7680]{0:T(1024)S(1)} all-reduce(f32[7680]{0:T(1024)S(1)} %constant_dynamic-update-slice_fusion.4), channel_id=7, replica_groups=mesh['rows'=8,'heads'=4] {'rows','heads'}, use_global_device_ids=true, to_apply=%region_35.36.clone | all-reduce | flops 7680 | bytes 61440
  651.5 21.2 %all-reduce.1 = f32[2,3,64]{2,1,0:T(4,128)S(1)} all-reduce(f32[2,3,64]{2,1,0:T(4,128)S(1)} %pad_maximum_fusion.1), channel_id=3, replica_groups=mesh['rows'=8,'heads'=4] {'rows'}, use_global_device_ids=true, to_apply=%region_20.21.clone | all-reduce | flops 384 | bytes 3072
  676.2 13.3 %copy.307 = bf16[3,1024,4,192]{1,3,2,0:T(8,128)(2,1)} copy(bf16[3,1024,4,192]{3,0,1,2:T(4,128)(2,1)} %bitcast.27) | data formatting | bytes 9437184 | tf_op jit(solution)/shard_map/all_to_all | solution.py:226
  692.1 8.9 bitcast_add_fusion
  703.4 125.8 %reduce-scatter.12.cloned.1.call-done = f32[96,768]{1,0:T(8,128)} async-done(((f32[3072,768]{1,0:T(8,128)}), f32[96,768]{1,0:T(8,128)}) %reduce-scatter.12.cloned.1.call-update) | async-done | bytes 294928 | tf_op jit(solution)/shard_map/reduce_scatter | solution.py:250
  832.3 3.6 copy.322
  835.9 39.8 %psum.7 = f32[]{:T(128)} all-reduce(f32[]{:T(128)S(6)} %add.277), channel_id=1, replica_groups=mesh['rows'=8,'heads'=4] {'rows','heads'}, use_global_device_ids=true, to_apply=%region_37.38 | all-reduce | flops 1 | bytes 8 | tf_op jit(solution)/shard_map/psum | solution.py:261
  884.2 2.3 multiply_add_fusion.1
  (286 shorter events, 152.7 us)
Async XLA Ops:
  8.0 40.5 %copy-start.11 = (f32[3,96,192]{2,1,0:T(8,128)S(1)}, f32[3,96,192]{2,1,0:T(8,128)}, u32[]{:S(2)}) copy-start(f32[3,96,192]{2,1,0:T(8,128)} %param.36) | copy-start | bytes 663556
  8.0 216.1 %all-gather.5.cloned.1.call-start = ((), (), s32[]{:S(2)}) async-start(), calls=%async_computation.7 | async-start | bytes 1216512 | tf_op jit(solution)/shard_map/all_gather | solution.py:165
  9.7 220.5 %all-gather.7.cloned.1.call-start = ((), (), s32[]{:S(2)}) async-start(), calls=%async_computation.8 | async-start | bytes 4866048 | tf_op jit(solution)/shard_map/all_gather | solution.py:166
  92.3 7.2 copy-start.8
  154.9 7.9 copy-start.4
  162.8 7.5 copy-start.13
  165.9 58.2 %all-to-all-start = ((bf16[4,1024,192]{1,2,0:T(8,128)(2,1)}), bf16[4,1024,192]{1,2,0:T(8,128)(2,1)}, u32[]{:S(2)}, u32[]{:S(2)}) async-start(bf16[4,1024,192]{1,2,0:T(8,128)(2,1)} %copy.294), calls=%async_computation | async-start | bytes 3145728 | tf_op jit(solution)/shard_map/all_to_all | solution.py:184
  170.3 97.6 %all-gather.9.cloned.1.call-start = ((), (), s32[]{:S(2)}) async-start(), calls=%async_computation.9 | async-start | bytes 4866048 | tf_op jit(solution)/shard_map/all_gather | solution.py:167
  171.1 3.3 copy-start.35
  171.1 52.2 %copy-start.9 = (bf16[1024,768]{1,0:T(8,128)(2,1)S(1)}, bf16[1024,768]{1,0:T(8,128)(2,1)}, u32[]{:S(2)}) copy-start(bf16[1024,768]{1,0:T(8,128)(2,1)} %param.33) | copy-start | bytes 4718596
  228.1 1.7 copy-start.2
  283.3 17.6 %copy-start.10 = (bf16[1024,768]{0,1:T(8,128)(2,1)}, bf16[1024,768]{0,1:T(8,128)(2,1)S(1)}, u32[]{:S(2)}) copy-start(bf16[1024,768]{0,1:T(8,128)(2,1)S(1)} %get-tuple-element.455) | copy-start | bytes 4718596
  300.8 11.0 %copy-start.3 = (f32[1024,768]{0,1:T(8,128)S(1)}, f32[1024,768]{0,1:T(8,128)}, u32[]{:S(2)}) copy-start(f32[1024,768]{0,1:T(8,128)} %copy-done.2) | copy-start | bytes 9437188
  312.6 4.7 copy-start
  312.6 2.1 copy-start.40
  317.3 23.6 %all-to-all-start.1 = ((bf16[1024,4,192]{0,2,1:T(8,128)(2,1)}), bf16[1024,4,192]{0,2,1:T(8,128)(2,1)S(1)}, u32[]{:S(2)}, u32[]{:S(2)}) async-start(bf16[1024,4,192]{0,2,1:T(8,128)(2,1)} %bitcast.23), calls=%async_computation.1 | async-start | bytes 3145728 | tf_op jit(solution)/shard_map/all_to_all | solution.py:212
  320.9 352.5 %reduce-scatter.8.cloned.1.call-start = ((), (), s32[]{:S(2)}) async-start(), calls=%async_computation.11 | async-start | bytes 2433024 | tf_op jit(solution)/shard_map/reduce_scatter | solution.py:248
  325.2 349.7 %reduce-scatter.14.cloned.1.call-start = ((), (), s32[]{:S(2)}) async-start(), calls=%async_computation.14 | async-start | bytes 2211840
  454.7 1.9 copy-start.6
  454.7 2.4 copy-start.7
  457.2 2.2 copy-start.5
  475.4 216.7 %all-gather.11.cloned.1.call-start = ((), (), s32[]{:S(2)}) async-start(), calls=%async_computation.10 | async-start | bytes 4423680 | tf_op jit(solution)/shard_map/all_gather | solution.py:227
  476.0 225.1 %reduce-scatter.10.cloned.1.call-start = ((), (), s32[]{:S(2)}) async-start(), calls=%async_computation.12 | async-start | bytes 9732096 | tf_op jit(solution)/shard_map/reduce_scatter | solution.py:249
  486.9 342.3 %reduce-scatter.12.cloned.1.call-start = ((), (), s32[]{:S(2)}) async-start(), calls=%async_computation.13 | async-start | bytes 9732096 | tf_op jit(solution)/shard_map/reduce_scatter | solution.py:250
  509.7 5.8 copy-start.12
  509.7 6.7 copy-start.41
  509.7 166.5 %all-to-all-start.2 = ((bf16[3,4096,192]{2,0,1:T(4,128)(2,1)}), bf16[3,4096,192]{2,0,1:T(4,128)(2,1)}, u32[]{:S(2)}, u32[]{:S(2)}) async-start(bf16[3,4096,192]{2,0,1:T(4,128)(2,1)} %copy.305), calls=%async_computation.2 | async-start | bytes 16777216 | tf_op jit(solution)/shard_map/all_to_all | solution.py:226
  650.3 25.7 %copy-start.30 = (f32[7680]{0:T(1024)}, f32[7680]{0:T(1024)S(1)}, u32[]{:S(2)}) copy-start(f32[7680]{0:T(1024)S(1)} %all-reduce.2) | copy-start | bytes 92164
  676.2 15.9 %copy-start.1 = (f32[1024,768]{0,1:T(8,128)S(1)}, f32[1024,768]{0,1:T(8,128)}, u32[]{:S(2)}) copy-start(f32[1024,768]{0,1:T(8,128)} %copy-done) | copy-start | bytes 9437188
  832.2 44.3 %copy-start.31 = (f32[2,3,8]{2,0,1:T(2,128)S(1)}, f32[2,3,8]{2,0,1:T(2,128)}, u32[]{:S(2)}) copy-start(f32[2,3,8]{2,0,1:T(2,128)} %param.40) | copy-start | bytes 580
  832.2 44.3 %copy-start.32 = (f32[2,3,8]{2,0,1:T(2,128)S(1)}, f32[2,3,8]{2,0,1:T(2,128)}, u32[]{:S(2)}) copy-start(f32[2,3,8]{2,0,1:T(2,128)} %param.43) | copy-start | bytes 580
  832.2 44.3 %copy-start.33 = (f32[2,3,8]{2,0,1:T(2,128)S(1)}, f32[2,3,8]{2,0,1:T(2,128)}, u32[]{:S(2)}) copy-start(f32[2,3,8]{2,0,1:T(2,128)} %param.41) | copy-start | bytes 580
  832.2 44.3 %copy-start.34 = (f32[2,3,8]{2,0,1:T(2,128)S(1)}, f32[2,3,8]{2,0,1:T(2,128)}, u32[]{:S(2)}) copy-start(f32[2,3,8]{2,0,1:T(2,128)} %param.42) | copy-start | bytes 580
  832.2 46.7 %copy-start.18 = (f32[3,96,192]{1,2,0:T(8,128)S(1)}, f32[3,96,192]{1,2,0:T(8,128)}, u32[]{:S(2)}) copy-start(f32[3,96,192]{1,2,0:T(8,128)} %copy.314) | copy-start | bytes 663556
  832.2 46.7 %copy-start.19 = (f32[3,96,192]{1,2,0:T(8,128)S(1)}, f32[3,96,192]{1,2,0:T(8,128)}, u32[]{:S(2)}) copy-start(f32[3,96,192]{1,2,0:T(8,128)} %copy.311) | copy-start | bytes 663556
  832.2 46.7 %copy-start.20 = (f32[3,96,192]{1,2,0:T(8,128)S(1)}, f32[3,96,192]{1,2,0:T(8,128)}, u32[]{:S(2)}) copy-start(f32[3,96,192]{1,2,0:T(8,128)} %copy.312) | copy-start | bytes 663556
  832.2 46.7 %copy-start.21 = (f32[3,96,192]{1,2,0:T(8,128)S(1)}, f32[3,96,192]{1,2,0:T(8,128)}, u32[]{:S(2)}) copy-start(f32[3,96,192]{1,2,0:T(8,128)} %copy.315) | copy-start | bytes 663556
  835.9 46.9 %copy-start.36 = (f32[240]{0:T(256)S(1)}, f32[240]{0:T(256)}, u32[]{:S(2)}) copy-start(f32[240]{0:T(256)} %param.56) | copy-start | bytes 2884
  835.9 46.9 %copy-start.37 = (f32[240]{0:T(256)S(1)}, f32[240]{0:T(256)}, u32[]{:S(2)}) copy-start(f32[240]{0:T(256)} %param.59) | copy-start | bytes 2884
  835.9 46.9 %copy-start.38 = (f32[240]{0:T(256)S(1)}, f32[240]{0:T(256)}, u32[]{:S(2)}) copy-start(f32[240]{0:T(256)} %param.57) | copy-start | bytes 2884
  835.9 46.9 %copy-start.39 = (f32[240]{0:T(256)S(1)}, f32[240]{0:T(256)}, u32[]{:S(2)}) copy-start(f32[240]{0:T(256)} %param.58) | copy-start | bytes 2884
  835.9 48.3 %copy-start.14 = (f32[96,768]{1,0:T(8,128)S(1)}, f32[96,768]{1,0:T(8,128)}, u32[]{:S(2)}) copy-start(f32[96,768]{1,0:T(8,128)} %param.52) | copy-start | bytes 884740
  835.9 48.3 %copy-start.17 = (f32[96,768]{1,0:T(8,128)S(1)}, f32[96,768]{1,0:T(8,128)}, u32[]{:S(2)}) copy-start(f32[96,768]{1,0:T(8,128)} %reduce-scatter.12.cloned.1.call-done) | copy-start | bytes 884740
  879.2 7.3 copy-start.15
  879.2 7.3 copy-start.16
  879.2 7.3 copy-start.24
  879.3 7.3 copy-start.25
  879.3 7.3 copy-start.26
  881.0 6.7 copy-start.22
  881.0 6.7 copy-start.23
  881.0 6.7 copy-start.27
  881.0 6.7 copy-start.28
  881.0 6.7 copy-start.29
Sparse Core Ops, SparseCore 0:
  12.4 60.2 all-gather.4
  76.2 63.6 all-gather.6
  174.6 62.7 all-gather.8
  326.7 100.0 reduce-scatter.7
  475.5 66.7 reduce-scatter.13
  548.1 139.5 reduce-scatter.9
  694.6 134.5 reduce-scatter.11
Sparse Core Ops, SparseCore 1:
  477.5 30.2 all-gather.10
where the time goes:
time: 911 us; the launch traced here: 898 us
  blocking collectives  307 us (34%)
  matrix products  236 us (26%)
  waiting for transfers between devices  142 us (16%)
  local copies, waits for them, and re-layouts  128 us (14%)
  other arithmetic  45.9 us (5%)
  between operations  23.3 us (3%)
  starting transfers between devices  14 us (2%)
    unnamed x3, blocking collectives  194 us
    reduce_scatter x1, waiting for transfers between devices, body(): lax.psum_scatter(grad_down, ('rows', 'heads'), scatter_dimension=0, tiled...  126 us
    unnamed x118, local copies, waits for them, and re-layouts  41.9 us
    all_gather x1, blocking collectives, body(): lax.all_gather(in_weight.astype(jnp.bfloat16), 'rows', axis=1, tiled=True)  41 us
    psum x1, blocking collectives, body(): grad_norm = jnp.sqrt(lax.psum(local_square, ('rows', 'heads')))  39.8 us
    dot_general x1, matrix products, body(): jnp.dot(first_low, gathered_up, preferred_element_type=jnp.float32)  37.8 us
    all_gather x1, blocking collectives, body(): lax.all_gather(in_bias.astype(jnp.bfloat16), 'rows', axis=2, tiled=True)  32.2 us
    dot_general x3, matrix products, contract_cols(): lax.dot_general(left, right, (((1,), (1,)), ((), ())), preferred_element_...  31.1 us
  transfers between devices with their start and end apart: 11, of which 2 were waited for; matrix products, arithmetic and copies ran while one was open for 37% of the time, Pallas kernels for 0%

commit v1 on v0

v1 whole, which is shorter than its diff:
```python
from functools import partial
import math

import jax
import jax.numpy as jnp
from jax import lax
from jax.experimental import pallas as pl
from jax.experimental.pallas import tpu as pltpu
from jax.sharding import PartitionSpec as P

D = 768
HD = 64
FF = 3072
CAP_L = 512
CAP_M = 128
CAP_S = 64
STEP = 10
ROWS_BLK = 8
PARAMS = 7087104

LN_EPS = 1e-05
LEARN_RATE = 0.1
VECTOR_RATE = 0.3
BETA_ONE = 0.9
BETA_TWO = 0.999
ADAM_EPS = 1e-08
WEIGHT_DECAY = 0.01
AVERAGE_KEEP = 0.75
CLIP_RMS = 0.001

AXES = ("rows", "heads")
BF = jnp.bfloat16
F32 = jnp.float32
VMEM_BYTES = 58 * 1024 * 1024
GROUP = 256
HALF = D // 2
PACK_VEC = 16


def dot_nn(left, right):
    return lax.dot_general(left, right, (((1,), (0,)), ((), ())), preferred_element_type=F32)


def dot_nt(left, right):
    return lax.dot_general(left, right, (((1,), (1,)), ((), ())), preferred_element_type=F32)


def dot_tn(left, right):
    return lax.dot_general(left, right, (((0,), (0,)), ((), ())), preferred_element_type=F32)


def kernel_params(steps=1):
    return pltpu.CompilerParams(
        vmem_limit_bytes=VMEM_BYTES, dimension_semantics=("arbitrary",) * steps
    )


def whole(shape):
    return pl.BlockSpec(shape, lambda *_: (0,) * len(shape))


ANY = pl.BlockSpec(memory_space=pl.ANY)


class Place:
    def __init__(self):
        self.n_rows = lax.axis_size("rows")
        self.n_heads = lax.axis_size("heads")
        self.total = self.n_rows * self.n_heads
        self.sizes = {"z": self.n_rows // 2, "y": 2, "x": self.n_heads // 2, "c": 2}
        self.strides = {"c": 1, "x": 2, "y": self.n_heads, "z": 2 * self.n_heads}
        row, head = lax.axis_index("rows"), lax.axis_index("heads")
        self.z, self.y = row // 2, row % 2
        self.x, self.c = head // 2, head % 2

    def send(self, value, digit, shift=1):
        size, stride = self.sizes[digit], self.strides[digit]
        pairs = []
        for device in range(self.total):
            own = (device // stride) % size
            pairs.append((device, device + ((own + shift) % size - own) * stride))
        return lax.ppermute(value, AXES, pairs)


def gather_pieces(place, piece):
    z_size = place.sizes["z"]
    column = jnp.stack([piece] + [place.send(piece, "z", shift) for shift in range(1, z_size)])
    from_x = place.send(column, "x")
    from_y = place.send(column, "y")
    cut = z_size // 2
    diag_low = place.send(from_x[:cut], "y")
    diag_high = place.send(from_y[cut:], "x")
    shifts = tuple(range(z_size))
    near = [
        (column, shifts, 0, 0, 0),
        (from_x, shifts, 0, 1, 0),
        (from_y, shifts, 1, 0, 0),
        (diag_low, shifts[:cut], 1, 1, 0),
        (diag_high, shifts[cut:], 1, 1, 0),
    ]
    far = [(place.send(buffer, "c"), s, y, x, 1) for buffer, s, y, x, _ in near]
    return near + far


def pick(value, index, axis):
    return lax.dynamic_index_in_dim(value, index, axis, keepdims=False)


def add_low(left, right):
    return (left.astype(F32) + right.astype(F32)).astype(BF)


def scatter_pair(place, value, digit, axis):
    own = getattr(place, digit)
    received = place.send(pick(value, 1 - own, axis), digit)
    return add_low(pick(value, own, axis), received)


def scatter_column(place, value):
    size = place.sizes["z"]
    total = pick(value, place.z, 0).astype(F32)
    for shift in range(1, size):
        part = place.send(pick(value, (place.z + shift) % size, 0), "z", shift)
        total = total + part.astype(F32)
    return total


def scatter_chip(place, value, x_first):
    if x_first:
        value = scatter_pair(place, value, "x", 2)
        value = scatter_pair(place, value, "y", 1)
    else:
        value = scatter_pair(place, value, "y", 1)
        value = scatter_pair(place, value, "x", 1)
    return scatter_column(place, value)


def swap_halves(place, value, cut_axis, join_axis):
    size = value.shape[cut_axis] // 2
    keep = lax.dynamic_slice_in_dim(value, place.c * size, size, cut_axis)
    give = lax.dynamic_slice_in_dim(value, (1 - place.c) * size, size, cut_axis)
    got = place.send(give, "c")
    first = jnp.where(place.c == 0, keep, got)
    second = jnp.where(place.c == 0, got, keep)
    return jnp.concatenate([first, second], axis=join_axis)


def sum_all(place, value):
    for digit in ("c", "x", "y"):
        value = value + place.send(value, digit)
    own = value
    for shift in range(1, place.sizes["z"]):
        value = value + place.send(own, "z", shift)
    return value


def run_copies(copies):
    for copy in copies:
        copy.start()
    return copies


def finish_copies(copies):
    for copy in copies:
        copy.wait()


def piece_origin(place_ref, z_size, entry, index):
    _, shifts, y, x, c = entry
    shift = shifts[index]
    z_at = lax.rem(place_ref[0] + (z_size - shift), z_size)
    return z_at, place_ref[1] ^ y, place_ref[2] ^ x, place_ref[3] ^ c


def lane_half(rows):
    return lax.broadcasted_iota(jnp.int32, (rows, 2 * HD), 1) < HD


def attend_kernel(layout, place_ref, x_ref, bias_ref, keys_ref, ones_ref, *rest):
    entries, z_size = layout
    n_in = len(entries) if entries else 1
    sources = rest[:n_in]
    q_ref, k_ref, v_ref, o_ref, lse_ref, weight, sems = rest[n_in:]
    group = pl.program_id(0)

    @pl.when(group == 0)
    def _():
        copies = []
        if entries:
            for entry, source in zip(entries, sources):
                for index in range(len(entry[1])):
                    z_at, y_at, x_at, c_at = piece_origin(place_ref, z_size, entry, index)
                    row = pl.multiple_of((z_at * 2 + y_at) * 96 + c_at * 48, 16)
                    col = pl.multiple_of(x_at * HALF, 128)
                    for j in range(3):
                        copies.append(
                            pltpu.make_async_copy(
                                source.at[index, pl.ds(j * 48, 48), :],
                                weight.at[j, pl.ds(row, 48), pl.ds(col, HALF)],
                                sems.at[len(copies)],
                            )
                        )
        else:
            copies.append(pltpu.make_async_copy(sources[0], weight, sems.at[0]))
        finish_copies(run_copies(copies))

    x = x_ref[...]
    at = pl.multiple_of(group * GROUP, GROUP)
    for j, out in enumerate((q_ref, k_ref, v_ref)):
        out[...] = (dot_nn(x, weight[j, :, pl.ds(at, GROUP)]) + bias_ref[j]).astype(BF)
    low = lane_half(CAP_L)
    for block in range(x_ref.shape[0] // CAP_L):
        rows = slice(block * CAP_L, (block + 1) * CAP_L)
        key_mask, query_row = keys_ref[rows, :], ones_ref[rows, :]
        for pair in range(GROUP // 128):
            cols = slice(pair * 128, (pair + 1) * 128)
            q2, k2 = q_ref[rows, cols] * BF(HD ** -0.5), k_ref[rows, cols]
            v2t = v_ref[rows, cols].T
            outs = []
            for side in range(2):
                here = low if side == 0 else ~low
                s = dot_nt(jnp.where(here, k2, key_mask), jnp.where(here, q2, query_row))
                peak = jnp.max(s, axis=0, keepdims=True)
                e = jnp.exp(s - peak)
                total = jnp.sum(e, axis=0, keepdims=True)
                o = dot_nn(v2t[side * HD : (side + 1) * HD], e.astype(BF))
                outs.append(o * (1.0 / total))
                slot = (block * (GROUP // 128) + pair) * 2 + side
                lse_ref[0, slot : slot + 1, :] = peak + jnp.log(total)
            o_ref[rows, cols] = jnp.concatenate(outs, axis=0).T.astype(BF)


def attend(place_vec, x, bias, key_mask, query_row, entries, buffers, z_size):
    tokens = x.shape[0]
    groups = D // GROUP
    slots = tokens // CAP_L * (GROUP // HD)
    n_copies = sum(3 * len(entry[1]) for entry in entries) if entries else 1
    layout = (entries, z_size)
    shape = jax.ShapeDtypeStruct((tokens, D), BF)
    block = pl.BlockSpec((tokens, GROUP), lambda g, p: (0, g))
    return pl.pallas_call(
        partial(attend_kernel, layout),
        grid_spec=pltpu.PrefetchScalarGridSpec(
            num_scalar_prefetch=1,
            grid=(groups,),
            in_specs=[
                whole((tokens, D)),
                pl.BlockSpec((3, 1, GROUP), lambda g, p: (0, 0, g)),
                whole((tokens, 128)),
                whole((tokens, 128)),
            ]
            + [ANY] * len(buffers),
            out_specs=[block] * 4 + [pl.BlockSpec((1, slots, CAP_L), lambda g, p: (g, 0, 0))],
            scratch_shapes=[pltpu.VMEM((3, D, D), BF), pltpu.SemaphoreType.DMA((n_copies,))],
        ),
        out_shape=[shape] * 4 + [jax.ShapeDtypeStruct((groups, slots, CAP_L), F32)],
        compiler_params=kernel_params(),
        cost_estimate=pl.CostEstimate(
            flops=8 * tokens * D * D, bytes_accessed=12 * tokens * D, transcendentals=0
        ),
        name="attend",
    )(place_vec, x, bias, key_mask, query_row, *buffers)


def attend_back_kernel(q_ref, k_ref, v_ref, do_ref, lse_ref, keys_ref, ones_ref, dq_ref, dk_ref, dv_ref, sum_ref):
    low = lane_half(CAP_L)
    sum_ref[...] = jnp.zeros_like(sum_ref)
    for block in range(q_ref.shape[0] // CAP_L):
        rows = slice(block * CAP_L, (block + 1) * CAP_L)
        key_mask, query_row = keys_ref[rows, :], ones_ref[rows, :]
        for pair in range(GROUP // 128):
            cols = slice(pair * 128, (pair + 1) * 128)
            q2, k2 = q_ref[rows, cols] * BF(HD ** -0.5), k_ref[rows, cols]
            v2, do2 = v_ref[rows, cols], do_ref[rows, cols]
            k2t = k2.T
            dq_t, dk, dv = [], [], []
            for side in range(2):
                here = low if side == 0 else ~low
                slot = (block * (GROUP // 128) + pair) * 2 + side
                s = dot_nt(jnp.where(here, k2, key_mask), jnp.where(here, q2, query_row))
                p = jnp.exp(s - lse_ref[0, slot : slot + 1, :])
                dp = dot_nt(jnp.where(here, v2, BF(0)), do2)
                dv.append(dot_nn(p.astype(BF), do2))
                inner = jnp.sum(dp * p, axis=0, keepdims=True)
                ds = (p * (dp - inner)).astype(BF)
                dk.append(dot_nn(ds, q2))
                dq_t.append(dot_nn(k2t[side * HD : (side + 1) * HD], ds))
            dq_low = (jnp.concatenate(dq_t, axis=0).T * HD ** -0.5).astype(BF)
            dv_low = jnp.where(low, dv[0], dv[1]).astype(BF)
            dq_ref[rows, cols] = dq_low
            dk_ref[rows, cols] = jnp.where(low, dk[0], dk[1]).astype(BF)
            dv_ref[rows, cols] = dv_low
            sum_ref[0:1, cols] += jnp.sum(dq_low.astype(F32), axis=0, keepdims=True)
            sum_ref[1:2, cols] += jnp.sum(dv_low.astype(F32), axis=0, keepdims=True)


def attend_back(q, k, v, do, lse, key_mask, query_row):
    tokens = q.shape[0]
    groups, slots, _ = lse.shape
    block = pl.BlockSpec((tokens, GROUP), lambda g: (0, g))
    shape = jax.ShapeDtypeStruct((tokens, D), BF)
    return pl.pallas_call(
        attend_back_kernel,
        grid=(groups,),
        in_specs=[block] * 4
        + [pl.BlockSpec((1, slots, CAP_L), lambda g: (g, 0, 0)), whole((tokens, 128)), whole((tokens, 128))],
        out_specs=[block] * 3 + [pl.BlockSpec((2, GROUP), lambda g: (0, g))],
        out_shape=[shape] * 3 + [jax.ShapeDtypeStruct((2, D), F32)],
        compiler_params=kernel_params(),
        cost_estimate=pl.CostEstimate(
            flops=20 * tokens * D * CAP_L, bytes_accessed=14 * tokens * D, transcendentals=0
        ),
        name="attend_back",
    )(q, k, v, do, lse, key_mask, query_row)


TILE = 512
CHUNK = 768
ERF_P = 0.3275911 / math.sqrt(2.0)
ERF_A = (0.254829592, -0.284496736, 1.421413741, -1.453152027, 1.061405429)


def gelu_parts(u):
    bell = jnp.exp(u * u * -0.5)
    t = 1.0 / (1.0 + ERF_P * jnp.abs(u))
    poly = ERF_A[4] * 0.5
    for term in ERF_A[3::-1]:
        poly = poly * t + term * 0.5
    below = poly * t * bell
    phi = jnp.where(u >= 0.0, 1.0 - below, below)
    return u * phi, phi + u * bell * (1.0 / math.sqrt(2.0 * math.pi))


def normalise(values):
    center = values - jnp.mean(values, axis=-1, keepdims=True)
    scale = lax.rsqrt(jnp.mean(center * center, axis=-1, keepdims=True) + LN_EPS)
    return center * scale, scale


def norm_back(grad, gain, normal, scale):
    inner = grad * gain
    first = jnp.mean(inner, axis=-1, keepdims=True)
    second = jnp.mean(inner * normal, axis=-1, keepdims=True)
    return (inner - first - normal * second) * scale


def col_sum(values):
    return jnp.sum(values.astype(F32), axis=0, keepdims=True)


def layer_kernel(layout, place_ref, o_ref, x_ref, cot_ref, vec_ref, b1_ref, *rest):
    entries, z_size, n_heads = layout
    n_in = len(entries) + 1 if entries else 3
    sources = rest[:n_in]
    (
        z_ref, dr1_ref, yr_ref, hr_ref, dur_ref, dfr_ref, dar_ref, dor_ref, sums_ref, db1_ref,
        wo, w1, w2, slope, sems,
    ) = rest[n_in:]

    @pl.when(pl.program_id(0) == 0)
    def _():
        sums_ref[...] = jnp.zeros_like(sums_ref)
        db1_ref[...] = jnp.zeros_like(db1_ref)
        copies = []

        def add(source, target):
            copies.append(pltpu.make_async_copy(source, target, sems.at[len(copies)]))

        if entries:
            for entry, source in zip(entries, sources):
                for index in range(len(entry[1])):
                    z_at, y_at, x_at, c_at = piece_origin(place_ref, z_size, entry, index)
                    row = pl.multiple_of(((z_at * 2 + y_at) * (n_heads // 2) + x_at) * 48, 16)
                    col = pl.multiple_of(c_at * HALF, 128)
                    add(source.at[index, pl.ds(144, 48), :], wo.at[pl.ds(row, 48), pl.ds(col, HALF)])
            for device in range(sources[-1].shape[0]):
                chip, core = device // 2, device % 2
                for part in range(2):
                    add(
                        sources[-1].at[device, part * 48 : (part + 1) * 48, :],
                        w1.at[chip * 48 : (chip + 1) * 48, pl.ds(core * (FF // 2) + part * D, D)],
                    )
                add(sources[-1].at[device, 96:192, :], w2.at[device * 96 : (device + 1) * 96, :])
        else:
            for source, target in zip(sources, (wo, w1, w2)):
                add(source, target)
        finish_copies(run_copies(copies))

    bo, b2, g1, c1, g2, c2 = (vec_ref[i : i + 1, :] for i in range(6))
    r1 = x_ref[...].astype(F32) + (dot_nn(o_ref[...], wo[...]) + bo)
    n1, scale1 = normalise(r1)
    y1 = n1 * g1 + c1
    yr = y1.astype(BF)
    yr_ref[...] = yr
    f = None
    for at in range(0, FF, CHUNK):
        cols = slice(at, at + CHUNK)
        u = dot_nn(yr, w1[:, cols]) + b1_ref[:, cols]
        act, grad = gelu_parts(u)
        act = act.astype(BF)
        hr_ref[:, cols] = act
        slope[:, cols] = grad
        part = dot_nn(act, w2[cols, :])
        f = part if f is None else f + part
    n2, scale2 = normalise(y1 + (f + b2))
    z_ref[...] = (n2 * g2 + c2).astype(BF)
    dz = cot_ref[...].astype(F32)
    dr2 = norm_back(dz, g2, n2, scale2)
    dfr = dr2.astype(BF)
    dfr_ref[...] = dfr
    sums_ref[1:2, :] += col_sum(dfr)
    sums_ref[4:5, :] += col_sum(dz * n2)
    sums_ref[5:6, :] += col_sum(dz)
    dy1 = dr2
    for at in range(0, FF, CHUNK):
        cols = slice(at, at + CHUNK)
        dur = (dot_nt(dfr, w2[cols, :]) * slope[:, cols]).astype(BF)
        dur_ref[:, cols] = dur
        db1_ref[:, cols] += col_sum(dur)
        dy1 = dy1 + dot_nt(dur, w1[:, cols])
    dr1 = norm_back(dy1, g1, n1, scale1)
    dr1_ref[...] = dr1
    dar = dr1.astype(BF)
    dar_ref[...] = dar
    sums_ref[0:1, :] += col_sum(dar)
    sums_ref[2:3, :] += col_sum(dy1 * n1)
    sums_ref[3:4, :] += col_sum(dy1)
    dor_ref[...] = dot_nt(dar, wo[...]).astype(BF)


def layer(place_vec, o, x, cotangent, vec, b1, entries, buffers, z_size, n_heads):
    tokens = x.shape[0]
    n_copies = sum(len(e[1]) for e in entries) + 3 * buffers[-1].shape[0] if entries else 3
    tile = pl.BlockSpec((TILE, D), lambda t, p: (t, 0))
    wide = pl.BlockSpec((TILE, FF), lambda t, p: (t, 0))
    low, full = jax.ShapeDtypeStruct((tokens, D), BF), jax.ShapeDtypeStruct((tokens, D), F32)
    low_wide = jax.ShapeDtypeStruct((tokens, FF), BF)
    return pl.pallas_call(
        partial(layer_kernel, (entries, z_size, n_heads)),
        grid_spec=pltpu.PrefetchScalarGridSpec(
            num_scalar_prefetch=1,
            grid=(tokens // TILE,),
            in_specs=[tile, tile, tile, whole((8, D)), whole((1, FF))] + [ANY] * len(buffers),
            out_specs=[tile, tile, tile, wide, wide, tile, tile, tile, whole((8, D)), whole((1, FF))],
            scratch_shapes=[
                pltpu.VMEM((D, D), BF),
                pltpu.VMEM((D, FF), BF),
                pltpu.VMEM((FF, D), BF),
                pltpu.VMEM((TILE, FF), F32),
                pltpu.SemaphoreType.DMA((n_copies,)),
            ],
        ),
        out_shape=[
            low, full, low, low_wide, low_wide, low, low, low,
            jax.ShapeDtypeStruct((8, D), F32), jax.ShapeDtypeStruct((1, FF), F32),
        ],
        compiler_params=kernel_params(),
        cost_estimate=pl.CostEstimate(
            flops=tokens * D * (4 * D + 8 * FF), bytes_accessed=tokens * (20 * D + 4 * FF), transcendentals=0
        ),
        name="layer",
    )(place_vec, o, x, cotangent, vec, b1, *buffers)


def outer_kernel(left_ref, right_ref, out_ref):
    out_ref[...] = dot_tn(left_ref[...], right_ref[...]).astype(BF)


def outer(left, right, tile_left, tile_right, name):
    tokens, rows = left.shape
    cols = right.shape[1]
    return pl.pallas_call(
        outer_kernel,
        grid=(rows // tile_left, cols // tile_right),
        in_specs=[
            pl.BlockSpec((tokens, tile_left), lambda i, j: (0, i)),
            pl.BlockSpec((tokens, tile_right), lambda i, j: (0, j)),
        ],
        out_specs=pl.BlockSpec((tile_left, tile_right), lambda i, j: (i, j)),
        out_shape=jax.ShapeDtypeStruct((rows, cols), BF),
        compiler_params=kernel_params(2),
        cost_estimate=pl.CostEstimate(
            flops=2 * tokens * rows * cols, bytes_accessed=2 * (tokens * (rows + cols) + rows * cols), transcendentals=0
        ),
        name=name,
    )(left, right)


def outer_three_kernel(x_ref, q_ref, k_ref, v_ref, out_ref):
    x = x_ref[...]
    for j, ref in enumerate((q_ref, k_ref, v_ref)):
        out_ref[j] = dot_tn(x, ref[...]).astype(BF)


def outer_three(x, dq, dk, dv):
    tokens = x.shape[0]
    block = pl.BlockSpec((tokens, GROUP), lambda g: (0, g))
    return pl.pallas_call(
        outer_three_kernel,
        grid=(D // GROUP,),
        in_specs=[whole((tokens, D))] + [block] * 3,
        out_specs=pl.BlockSpec((3, D, GROUP), lambda g: (0, 0, g)),
        out_shape=jax.ShapeDtypeStruct((3, D, D), BF),
        compiler_params=kernel_params(),
        cost_estimate=pl.CostEstimate(
            flops=6 * tokens * D * D, bytes_accessed=8 * tokens * D + 6 * D * D, transcendentals=0
        ),
        name="grad_in",
    )(x, dq, dk, dv)


def input_grad_kernel(layout, place_ref, dr1_ref, dq_ref, dk_ref, dv_ref, *rest):
    entries, z_size = layout
    n_in = len(entries) if entries else 1
    sources = rest[:n_in]
    out_ref, weight, sems = rest[n_in:]

    @pl.when(pl.program_id(0) == 0)
    def _():
        copies = []
        if entries:
            for entry, source in zip(entries, sources):
                for index in range(len(entry[1])):
                    z_at, y_at, x_at, c_at = piece_origin(place_ref, z_size, entry, index)
                    row = pl.multiple_of((z_at * 2 + y_at) * 96 + c_at * 48, 16)
                    col = pl.multiple_of(x_at * HALF, 128)
                    for j in range(3):
                        copies.append(
                            pltpu.make_async_copy(
                                source.at[index, pl.ds(j * 48, 48), :],
                                weight.at[j, pl.ds(row, 48), pl.ds(col, HALF)],
                                sems.at[len(copies)],
                            )
                        )
        else:
            copies.append(pltpu.make_async_copy(sources[0], weight, sems.at[0]))
        finish_copies(run_copies(copies))

    total = dr1_ref[...]
    for j, ref in enumerate((dq_ref, dk_ref, dv_ref)):
        total = total + dot_nt(ref[...], weight[j])
    out_ref[...] = total


def input_grad(place_vec, dr1, dq, dk, dv, entries, buffers, z_size):
    tokens = dr1.shape[0]
    n_copies = sum(3 * len(entry[1]) for entry in entries) if entries else 1
    tile = pl.BlockSpec((TILE, D), lambda t, p: (t, 0))
    return pl.pallas_call(
        partial(input_grad_kernel, (entries, z_size)),
        grid_spec=pltpu.PrefetchScalarGridSpec(
            num_scalar_prefetch=1,
            grid=(tokens // TILE,),
            in_specs=[tile] * 4 + [ANY] * len(buffers),
            out_specs=tile,
            scratch_shapes=[pltpu.VMEM((3, D, D), BF), pltpu.SemaphoreType.DMA((n_copies,))],
        ),
        out_shape=jax.ShapeDtypeStruct((tokens, D), F32),
        compiler_params=kernel_params(),
        cost_estimate=pl.CostEstimate(
            flops=6 * tokens * D * D, bytes_accessed=14 * tokens * D + 6 * D * D, transcendentals=0
        ),
        name="input_grad",
    )(place_vec, dr1, dq, dk, dv, *buffers)


def mask_columns(kinds, lengths):
    capacity = jnp.where(kinds == 0, CAP_L, jnp.where(kinds == 1, CAP_M, CAP_S)).astype(jnp.int32)
    place = jnp.arange(CAP_L, dtype=jnp.int32)[None, :]
    row = place // capacity[:, None]
    within = place - row * capacity[:, None]
    lane = jnp.arange(2 * HD, dtype=jnp.int32) % HD
    same = row[:, :, None] == lane[None, None, :]
    padded = jnp.pad(lengths, ((0, 0), (0, HD - ROWS_BLK)))
    padded = jnp.concatenate([padded, padded], axis=1)
    live = same & (within[:, :, None] < padded[:, None, :])
    used = (lane < ROWS_BLK)[None, None, :]
    keys = jnp.where(live | ~used, 0.0, -1e30).astype(BF)
    queries = jnp.where(same & used, 1.0, 0.0).astype(BF)
    tokens = kinds.shape[0] * CAP_L
    return keys.reshape(tokens, 2 * HD), queries.reshape(tokens, 2 * HD)


def split_vector(vec_values):
    split_points = [D, D + FF, 2 * D + FF, 3 * D + FF, 4 * D + FF, 5 * D + FF]
    return jnp.split(vec_values, split_points)


def adam_update(weight, first, second, average, gradient, rate):
    first_new = BETA_ONE * first + (1.0 - BETA_ONE) * gradient
    second_new = BETA_TWO * second + (1.0 - BETA_TWO) * gradient * gradient
    first_hat = first_new / (1.0 - BETA_ONE**STEP)
    second_hat = second_new / (1.0 - BETA_TWO**STEP)
    weight_new = weight - rate * (
        first_hat / (jnp.sqrt(second_hat) + ADAM_EPS) + WEIGHT_DECAY * weight
    )
    average_new = AVERAGE_KEEP * average + (1.0 - AVERAGE_KEEP) * weight_new
    return (weight_new, first_new, second_new, average_new)


def body(
    tokens,
    cotangent,
    bucket,
    lengths,
    in_weight,
    in_first,
    in_second,
    in_average,
    in_bias,
    bias_first,
    bias_second,
    bias_average,
    out_weight,
    out_first,
    out_second,
    out_average,
    up_weight,
    up_first,
    up_second,
    up_average,
    down_weight,
    down_first,
    down_second,
    down_average,
    vectors,
    vec_first,
    vec_second,
    vec_average,
):
    place = Place()
    n_rows, n_heads, total = place.n_rows, place.n_heads, place.total
    z_size = place.sizes["z"]
    share = cotangent.shape[0]
    head_index = lax.axis_index("heads")
    place_vec = jnp.stack([place.z, place.y, place.x, place.c]).astype(jnp.int32)
    in_rows, in_cols = in_weight.shape[1], in_weight.shape[2]
    out_rows, down_rows = out_weight.shape[0], down_weight.shape[0]
    bias_len, vec_len = in_bias.size, vectors.size
    pieces_fit = in_rows == 96 and in_cols == HALF // 2 and out_rows == 24 and n_heads == 4

    small = jnp.concatenate([vectors, in_bias.reshape(-1)]).astype(BF)
    if pieces_fit:
        low_in = swap_halves(place, in_weight.astype(BF), 1, 2)
        low_out = swap_halves(place, out_weight.astype(BF), 1, 0)
        low_up = swap_halves(place, up_weight.astype(BF), 1, 0)
        small_rows = jnp.pad(small[None, :], ((0, PACK_VEC - 1), (0, HALF - small.size)))
        piece = jnp.concatenate([low_in.reshape(3 * 48, HALF), low_out, small_rows], axis=0)
        entries = gather_pieces(place, piece)
        ffn_piece = jnp.concatenate([low_up[:, :D], low_up[:, D:], down_weight.astype(BF)], axis=0)
        ffn_all = lax.all_gather(ffn_piece, AXES, axis=0)
        buffers = [entry[0] for entry in entries]
        layout = [(None,) + entry[1:] for entry in entries]
        in_buffers, layer_buffers = buffers, buffers + [ffn_all]
        found, origin = [], []
        for buffer, shifts, y, x, c in entries:
            for index, shift in enumerate(shifts):
                found.append(buffer[index, 3 * 48 + 48, : small.size])
                z_at = (place.z + z_size - shift) % z_size
                origin.append(
                    ((z_at * 2 + (place.y ^ y)) * 2 + (place.x ^ x)) * 2 + (place.c ^ c)
                )
        hit = jnp.stack(origin)[None, :] == jnp.arange(total, dtype=jnp.int32)[:, None]
        all_small = jnp.dot(hit.astype(BF), jnp.stack(found), preferred_element_type=F32)
    else:
        layout = ()
        all_in = lax.all_gather(in_weight.astype(BF), "rows", axis=1, tiled=True)
        all_in = lax.all_gather(all_in, "heads", axis=2, tiled=True)
        all_out, all_up, all_down = (
            lax.all_gather(w.astype(BF), AXES, axis=0, tiled=True)
            for w in (out_weight, up_weight, down_weight)
        )
        in_buffers, layer_buffers = [all_in], [all_out, all_up, all_down]
        all_small = lax.all_gather(small, AXES, axis=0).astype(F32)

    bias_out, bias_up, bias_down, gain_one, shift_one, gain_two, shift_two = split_vector(
        all_small[:, :vec_len].reshape(-1)
    )
    bias_shape = (n_rows, n_heads) + in_bias.shape
    bias_all = all_small[:, vec_len:].reshape(bias_shape).transpose(2, 1, 3, 0, 4).reshape(2, D)
    bias_in = jnp.stack([bias_all[0], jnp.zeros_like(bias_all[0]), bias_all[1]])[:, None, :]
    vec_rows = jnp.stack([bias_out, bias_down, gain_one, shift_one, gain_two, shift_two, bias_out, bias_out])

    x = lax.dynamic_slice_in_dim(tokens, head_index * share, share, 0)
    blocks = share // CAP_L
    own_kinds = lax.dynamic_slice_in_dim(bucket, head_index * blocks, blocks, 0)
    own_lengths = lax.dynamic_slice_in_dim(lengths, head_index * blocks, blocks, 0)
    key_mask, query_row = mask_columns(own_kinds, own_lengths)

    q, k, v, o, lse = attend(place_vec, x, bias_in, key_mask, query_row, layout, in_buffers, z_size)
    layer_out, dr1, yr, hr, dur, dfr, dar, dor, sums, db1 = layer(
        place_vec, o, x, cotangent, vec_rows, bias_up[None, :], layout, layer_buffers, z_size, n_heads
    )
    grad_down = outer(hr, dfr, D, D, "grad_down")
    grad_up = outer(yr, dur, D, D, "grad_up")
    grad_out = outer(o, dar, D, D // 2, "grad_out")
    dq, dk, dv, bias_sums = attend_back(q, k, v, dor, lse, key_mask, query_row)
    grad_in = outer_three(x, dq, dk, dv)
    token_grad = input_grad(place_vec, dr1, dq, dk, dv, layout, in_buffers, z_size)

    grad_vec = jnp.concatenate([sums[0], db1[0], sums[1], sums[2], sums[3], sums[4], sums[5]])
    grad_vec = grad_vec.reshape(total, vec_len)
    grad_bias = bias_sums.reshape(2, n_heads, in_bias.shape[1], n_rows, in_bias.shape[2])
    grad_bias = grad_bias.transpose(3, 1, 0, 2, 4).reshape(total, bias_len)
    grad_small = jnp.concatenate([grad_vec, grad_bias], axis=1)
    if pieces_fit:
        def core_pair(value, axis):
            return scatter_pair(place, value, "c", axis)

        down = core_pair(grad_down.reshape(z_size, 2, 2, 2, down_rows, D), 3)
        sum_down = scatter_chip(place, down, True)
        up = core_pair(grad_up.reshape(z_size, 2, 2, 48, 2, FF // 2), 4)
        sum_up = swap_halves(place, scatter_chip(place, up, False), 0, 1)
        send_out = grad_out.reshape(z_size, 2, 2, 48, 2, HALF)
        send_in = grad_in.reshape(3, z_size, 2, 2, 48, 2, HALF)
        send_small = jnp.pad(grad_small.astype(BF), ((0, 0), (0, HALF - small.size)))
        send_small = send_small.reshape(z_size, 2, 2, 2, 1, HALF)

        def packed(core):
            part_in = pick(send_in, core, 3).transpose(1, 2, 4, 0, 3, 5)
            part_in = part_in.reshape(z_size, 2, 2, 144, HALF)
            part_small = jnp.pad(pick(send_small, core, 3), ((0, 0),) * 3 + ((0, PACK_VEC - 1), (0, 0)))
            return jnp.concatenate([part_in, pick(send_out, core, 4), part_small], axis=3)

        mixed = add_low(packed(place.c), place.send(packed(1 - place.c), "c"))
        mixed = scatter_chip(place, mixed, True)
        sum_in = swap_halves(place, mixed[:144].reshape(3, 48, HALF), 2, 1)
        sum_out = swap_halves(place, mixed[144:192], 0, 1)
        sum_small = mixed[192, : small.size]
    else:
        def spread(value):
            return lax.psum_scatter(value, AXES, scatter_dimension=0, tiled=True).astype(F32)

        sum_in = lax.psum_scatter(grad_in, "heads", scatter_dimension=2, tiled=True)
        sum_in = lax.psum_scatter(sum_in, "rows", scatter_dimension=1, tiled=True).astype(F32)
        sum_out, sum_up, sum_down = spread(grad_out), spread(grad_up), spread(grad_down)
        sum_small = lax.psum_scatter(grad_small, AXES, scatter_dimension=0, tiled=True)[0]
    sum_vec = sum_small[:vec_len]
    sum_bias = sum_small[vec_len:].reshape(in_bias.shape)

    local_square = (
        jnp.sum(sum_in * sum_in)
        + jnp.sum(sum_out * sum_out)
        + jnp.sum(sum_up * sum_up)
        + jnp.sum(sum_down * sum_down)
        + jnp.sum(sum_small * sum_small)
    )
    grad_norm = jnp.sqrt(sum_all(place, local_square))
    clip_limit = CLIP_RMS * math.sqrt(PARAMS)
    factor = clip_limit / jnp.maximum(grad_norm, clip_limit)
    in_new = adam_update(in_weight, in_first, in_second, in_average, sum_in * factor, LEARN_RATE)
    bias_new = adam_update(
        in_bias, bias_first, bias_second, bias_average, sum_bias * factor, LEARN_RATE
    )
    out_new = adam_update(
        out_weight, out_first, out_second, out_average, sum_out * factor, LEARN_RATE
    )
    up_new = adam_update(up_weight, up_first, up_second, up_average, sum_up * factor, LEARN_RATE)
    down_new = adam_update(
        down_weight, down_first, down_second, down_average, sum_down * factor, LEARN_RATE
    )
    vec_new = adam_update(
        vectors, vec_first, vec_second, vec_average, sum_vec * factor, VECTOR_RATE
    )
    return (
        layer_out,
        token_grad,
        grad_norm,
        *in_new,
        *bias_new,
        *out_new,
        *up_new,
        *down_new,
        *vec_new,
    )


def solution(mesh):
    in_specs = (
        P("rows", None),
        P(("rows", "heads"), None),
        P("rows"),
        P("rows", None),
        P(None, "rows", "heads"),
        P(None, "rows", "heads"),
        P(None, "rows", "heads"),
        P(None, "rows", "heads"),
        P(None, "heads", "rows"),
        P(None, "heads", "rows"),
        P(None, "heads", "rows"),
        P(None, "heads", "rows"),
        P(("rows", "heads"), None),
        P(("rows", "heads"), None),
        P(("rows", "heads"), None),
        P(("rows", "heads"), None),
        P(("rows", "heads"), None),
        P(("rows", "heads"), None),
        P(("rows", "heads"), None),
        P(("rows", "heads"), None),
        P(("rows", "heads"), None),
        P(("rows", "heads"), None),
        P(("rows", "heads"), None),
        P(("rows", "heads"), None),
        P(("rows", "heads")),
        P(("rows", "heads")),
        P(("rows", "heads")),
        P(("rows", "heads")),
    )
    out_specs = (
        P(("rows", "heads"), None),
        P(("rows", "heads"), None),
        P(),
        P(None, "rows", "heads"),
        P(None, "rows", "heads"),
        P(None, "rows", "heads"),
        P(None, "rows", "heads"),
        P(None, "heads", "rows"),
        P(None, "heads", "rows"),
        P(None, "heads", "rows"),
        P(None, "heads", "rows"),
        P(("rows", "heads"), None),
        P(("rows", "heads"), None),
        P(("rows", "heads"), None),
        P(("rows", "heads"), None),
        P(("rows", "heads"), None),
        P(("rows", "heads"), None),
        P(("rows", "heads"), None),
        P(("rows", "heads"), None),
        P(("rows", "heads"), None),
        P(("rows", "heads"), None),
        P(("rows", "heads"), None),
        P(("rows", "heads"), None),
        P(("rows", "heads")),
        P(("rows", "heads")),
        P(("rows", "heads")),
        P(("rows", "heads")),
    )
    return jax.shard_map(body, mesh=mesh, in_specs=in_specs, out_specs=out_specs, check_vma=False)
```

time: 911 us -> 457 us (0.50)
  blocking collectives: 307 us -> 0 us
  matrix products: 236 us -> 0.13 us
  Pallas kernels: 0 us -> 146 us
  local copies, waits for them, and re-layouts: 128 us -> 68.7 us
  starting transfers between devices: 14 us -> 61.5 us
  waiting for transfers between devices: 142 us -> 119 us
  other arithmetic: 45.9 us -> 29.6 us
    dot_general x68 -> x1, matrix products: 236 us -> 0.13 us  [body(): jnp.dot(hit.astype(BF), jnp.stack(found), preferred_element_type=F32)]
    unnamed x3 -> x0, blocking collectives: 194 us -> none
    pallas_call x0 -> x8, Pallas kernels: none -> 146 us  [the longest x1 59 us: layer(): pl.pallas_call(partial(layer_kernel, (entries, z_size, n_heads)), grid_sp...]
    reduce_scatter x3 -> x0, waiting for transfers between devices: 126 us -> none  [the longest x1 126 us: body(): lax.psum_scatter(grad_down, ('rows', 'heads'), scatter_dimension=0, tiled...]
    ppermute x0 -> x42, waiting for transfers between devices: none -> 108 us  [send(): return lax.ppermute(value, AXES, pairs)]
    all_gather x2 -> x0, blocking collectives: 73.2 us -> none  [the longest x1 41 us: body(): lax.all_gather(in_weight.astype(jnp.bfloat16), 'rows', axis=1, tiled=True)]
    ppermute x0 -> x42, starting transfers between devices: none -> 61.4 us  [send(): return lax.ppermute(value, AXES, pairs)]
    psum x1 -> x0, blocking collectives: 39.8 us -> none  [body(): grad_norm = jnp.sqrt(lax.psum(local_square, ('rows', 'heads')))]
  transfers between devices with their start and end apart: 11 -> 43, of which waited for: 2 -> 24; matrix products, arithmetic and copies ran while one was open for 37% -> 18% of each run, Pallas kernels for 0% -> 17%
where the time goes in v1:
time: 457 us; the launch traced here: 449 us
  Pallas kernels  146 us (32%)
  waiting for transfers between devices  119 us (26%)
  local copies, waits for them, and re-layouts  68.7 us (15%)
  starting transfers between devices  61.5 us (13%)
  other arithmetic  29.6 us (6%)
  between operations  24 us (5%)
    ppermute x42, waiting for transfers between devices, send(): return lax.ppermute(value, AXES, pairs)  108 us
    ppermute x42, starting transfers between devices, send(): return lax.ppermute(value, AXES, pairs)  61.4 us
    pallas_call x1, Pallas kernels, layer(): pl.pallas_call(partial(layer_kernel, (entries, z_size, n_heads)), grid_sp...  59 us
    dynamic_slice x9, local copies, waits for them, and re-layouts, pick(): return lax.dynamic_index_in_dim(value, index, axis, keepdims=False)  30.6 us
    pallas_call x1, Pallas kernels, attend(): pl.pallas_call(partial(attend_kernel, layout), grid_spec=pltpu.PrefetchSc...  23.1 us
    pallas_call x3, Pallas kernels, outer(): pl.pallas_call(outer_kernel, grid=(rows // tile_left, cols // tile_right)...  22.9 us
    pallas_call x1, Pallas kernels, attend_back(): pl.pallas_call(attend_back_kernel, grid=(groups,), in_specs=[block] * 4 +...  21.4 us
    convert_element_type x9, other arithmetic, add_low(): return (left.astype(F32) + right.astype(F32)).astype(BF)  12.7 us
  transfers between devices with their start and end apart: 43, of which 24 were waited for; matrix products, arithmetic and copies ran while one was open for 18% of the time, Pallas kernels for 17%

profile of v1, /device:TPU:0, one launch (start us, length us, event | category | flops | bytes accessed | tf_op | source)
XLA Modules:
  0.0 449.3 jit_solution(8451134656455999666)
XLA Ops:
  12.0 2.7 constant_dynamic-slice_fusion.17.x_ref
  17.0 2.9 collective-permute-start.2
  19.8 2.6 collective-permute-start.3
  22.4 1.3 collective-permute-start.4
  23.8 3.1 collective-permute-done.2
  26.8 11.0 %collective-permute-done.3 = bf16[208,384]{1,0:T(8,128)(2,1)S(1)} collective-permute-done((bf16[208,384]{1,0:T(8,128)(2,1)S(1)}, bf16[208,384]{1,0:T(8,128)(2,1)S(1)}, u32[]{:S(2)}, u32[]{:S(2)}) %collective-permute-start.3) | collective-permute-done | bytes 159776 | tf_op jit(solution)/shard_map/ppermute | solution.py:82
  38.0 1.7 collective-permute-start.6
  39.7 1.5 collective-permute-start.5
  41.3 17.2 %collective-permute-done.6.rest_2_ = bf16[4,208,384]{2,1,0:T(8,128)(2,1)S(1)} collective-permute-done((bf16[4,208,384]{2,1,0:T(8,128)(2,1)S(1)}, bf16[4,208,384]{2,1,0:T(8,128)(2,1)S(1)}, u32[]{:S(2)}, u32[]{:S(2)}) %collective-permute-start.6) | collective-permute-done | bytes 639008 | tf_op jit(solution)/shard_map/ppermute | solution.py:82
  58.5 1.6 collective-permute-start.8
  60.1 3.9 collective-permute-done.5.rest_1_
  64.7 6.1 %collective-permute-done.8.rest_4_ = bf16[2,208,384]{2,1,0:T(8,128)(2,1)S(1)} collective-permute-done((bf16[2,208,384]{2,1,0:T(8,128)(2,1)S(1)}, bf16[2,208,384]{2,1,0:T(8,128)(2,1)S(1)}, u32[]{:S(2)}, u32[]{:S(2)}) %collective-permute-start.8) | collective-permute-done | bytes 319520 | tf_op jit(solution)/shard_map/ppermute | solution.py:82
  76.8 23.1 %attend.1 = (bf16[1024,768]{1,0:T(8,128)(2,1)}, bf16[1024,768]{1,0:T(8,128)(2,1)}, bf16[1024,768]{1,0:T(8,128)(2,1)}, bf16[1024,768]{1,0:T(8,128)(2,1)}, f32[3,8,512]{2,1,0:T(8,128)}) custom-call(s32[4]{0:T(128)} %pad_add_fusion.1.place_ref, bf16[1024,768]{1,0:T(8,128)(2,1)} %constant_dynamic-slice_fusion.17.x_ref, f32[3,1,768]{2,1,0:T(1,128)} %broadcast_in_dim.41.bias_ref, ...), custom_call_target="tpu_custom_call" | custom-call | flops 4831838208 | bytes 9437184 | tf_op jit(solution)/shard_map/attend/pallas_call | solution.py:241
  99.9 11.7 %all-gather.3.cloned.1.call-done = bf16[6144,768]{1,0:T(8,128)(2,1)} async-done(((bf16[192,768]{1,0:T(8,128)(2,1)}), bf16[6144,768]{1,0:T(8,128)(2,1)}) %all-gather.3.cloned.1.call-update) | async-done | bytes 9437200 | tf_op jit(solution)/shard_map/all_gather | solution.py:651
  111.6 59.0 %layer.1 = (bf16[1024,768]{1,0:T(8,128)(2,1)}, f32[1024,768]{1,0:T(8,128)}, bf16[1024,768]{1,0:T(8,128)(2,1)}, bf16[1024,3072]{1,0:T(8,128)(2,1)}, bf16[1024,307...) custom-call(s32[4]{0:T(128)} %pad_add_fusion.1.place_ref, ...), custom_call_target="tpu_custom_call" | custom-call | flops 21743271936 | bytes 28311552 | tf_op jit(solution)/shard_map/layer/pallas_call | solution.py:438
  170.5 9.2 %grad_down.1 = bf16[3072,768]{1,0:T(8,128)(2,1)} custom-call(bf16[1024,3072]{1,0:T(8,128)(2,1)} %get-tuple-element.63.left_ref, bf16[1024,768]{1,0:T(8,128)(2,1)} %get-tuple-element.64.right_ref), custom_call_target="tpu_custom_call" | custom-call | flops 4831838208 | bytes 12582912 | tf_op jit(solution)/shard_map/grad_down/pallas_call | solution.py:472
  179.7 4.1 constant_dynamic-slice_fusion.1
  183.8 1.6 copy.141
  185.7 9.2 %grad_up.1 = bf16[768,3072]{1,0:T(8,128)(2,1)} custom-call(bf16[1024,768]{1,0:T(8,128)(2,1)} %get-tuple-element.61.left_ref, bf16[1024,3072]{1,0:T(8,128)(2,1)} %get-tuple-element.62.right_ref), custom_call_target="tpu_custom_call" | custom-call | flops 4831838208 | bytes 12582912 | tf_op jit(solution)/shard_map/grad_up/pallas_call | solution.py:472
  194.9 11.7 %reshape.338 = bf16[4,2,2,48,2,1536]{5,4,3,2,1,0:T(2,128)(2,1)} reshape(bf16[768,3072]{1,0:T(8,128)(2,1)} %grad_up.1) | data formatting | bytes 9437184 | tf_op jit(solution)/shard_map/reshape | solution.py:712
  206.5 13.7 %constant_dynamic-slice_fusion.4 = (bf16[4,2,2,48,1,1536]{5,4,3,2,1,0:T(2,128)(2,1)}, bf16[4,2,2,48,1,1536]{5,4,3,2,1,0:T(2,128)(2,1)S(1)}) fusion(bf16[4,2,2,48,2,1536]{5,4,3,2,1,0:T(2,128)(2,1)} %reshape.338, s32[]{:T(128)S(6)} %select_n.361, s32[]{:T(128)S(6)} %select_n.362), kind=kLoop, calls=%fused_computation.129 | loop fusion | bytes 9437192 | tf_op jit(solution)/shard_map/jit(dynamic_index_in_dim)/dynamic_slice | solution.py:106
  220.2 2.1 copy.142
  222.5 21.4 %attend_back.1 = (bf16[1024,768]{1,0:T(8,128)(2,1)}, bf16[1024,768]{1,0:T(8,128)(2,1)}, bf16[1024,768]{1,0:T(8,128)(2,1)}, f32[2,768]{1,0:T(2,128)}) custom-call(bf16[1024,768]{1,0:T(8,128)(2,1)} %get-tuple-element.49.q_ref, bf16[1024,768]{1,0:T(8,128)(2,1)} %get-tuple-element.50.k_ref, bf16[1024,768]{1,0:T(8,128)(2,1)} %get-tuple-element.51.v_ref, ...), custom_call_target="tpu_custom_call" | custom-call | flops 8053063680 | bytes 11010048 | tf_op jit(solution)/shard_map/attend_back/pallas_call | solution.py:302
  243.9 8.1 %grad_in.1 = bf16[3,768,768]{2,1,0:T(8,128)(2,1)} custom-call(bf16[1024,768]{1,0:T(8,128)(2,1)} %constant_dynamic-slice_fusion.17.x_ref, bf16[1024,768]{1,0:T(8,128)(2,1)} %get-tuple-element.54.dq_ref.q_ref, bf16[1024,768]{1,0:T(8,128)(2,1)} %get-tuple-element.55.dk_ref.k_ref, bf16[1024,768]{1,0:T(8,128)(2,1)} %get-tuple-element.56.dv_ref.v_ref), custom_call_target="tpu_custom_call" | custom-call | flops 3623878656 | bytes 9830400 | tf_op jit(solution)/shard_map/grad_in/pallas_call | solution.py:498
  252.0 6.6 %reshape.329 = bf16[3,4,2,2,48,2,384]{6,5,4,3,2,1,0:T(2,128)(2,1)S(1)} reshape(bf16[3,768,768]{2,1,0:T(8,128)(2,1)} %grad_in.1) | data formatting | bytes 7077888 | tf_op jit(solution)/shard_map/reshape | solution.py:715
  258.6 3.7 constant_dynamic-slice_fusion.12
  262.5 4.5 %grad_out.1 = bf16[768,768]{1,0:T(8,128)(2,1)} custom-call(bf16[1024,768]{1,0:T(8,128)(2,1)} %get-tuple-element.46.o_ref.left_ref, bf16[1024,768]{1,0:T(8,128)(2,1)} %get-tuple-element.57.right_ref), custom_call_target="tpu_custom_call" | custom-call | flops 1207959552 | bytes 4325376 | tf_op jit(solution)/shard_map/grad_out/pallas_call | solution.py:472
  267.0 3.0 reshape.331
  270.1 3.9 constant_dynamic-slice_fusion.11
  277.8 2.9 fusion.5
  282.1 4.0 fusion.3
  286.1 1.2 dynamic-slice_bitcast_fusion.2
  287.4 1.5 collective-permute-start.24
  289.1 2.4 fusion.2
  292.6 1.4 collective-permute-start.31
  294.0 2.0 add_convert_fusion
  297.9 11.4 %input_grad.1 = f32[1024,768]{1,0:T(8,128)} custom-call(s32[4]{0:T(128)} %pad_add_fusion.1.place_ref, f32[1024,768]{1,0:T(8,128)} %get-tuple-element.48.dr1_ref, bf16[1024,768]{1,0:T(8,128)(2,1)} %get-tuple-element.54.dq_ref.q_ref, bf16[1024,768]{1,0:T(8,128)(2,1)} %get-tuple-element.55.dk_ref.k_ref, bf16[1024,768]{1,0:T(8,128)(2,1)} %get-tuple-element.56.dv_ref.v_ref, ...), custom_call_target="tpu_custom_call" | custom-call | flops 3623878656 | bytes 14548992 | tf_op jit(solution)/shard_map/input_grad/pallas_call | solution.py:549
  309.3 6.5 %collective-permute-done.24 = bf16[4,2,48,1536]{3,2,0,1:T(8,128)(2,1)} collective-permute-done((bf16[4,2,48,1536]{3,2,0,1:T(8,128)(2,1)}, bf16[4,2,48,1536]{3,2,0,1:T(8,128)(2,1)}, u32[]{:S(2)}, u32[]{:S(2)}) %collective-permute-start.24) | collective-permute-done | bytes 1179680 | tf_op jit(solution)/shard_map/ppermute | solution.py:82
  315.8 1.9 fusion.8
  317.8 1.5 collective-permute-start.25
  319.3 2.4 collective-permute-done.31
  321.7 1.6 fusion.7
  323.3 1.5 collective-permute-start.32
  324.9 24.1 %collective-permute-done.16 = bf16[4,2,208,384]{3,2,0,1:T(8,128)(2,1)S(1)} collective-permute-done((bf16[4,2,208,384]{3,2,0,1:T(8,128)(2,1)}, bf16[4,2,208,384]{3,2,0,1:T(8,128)(2,1)S(1)}, u32[]{:S(2)}, u32[]{:S(2)}) %collective-permute-start.16) | collective-permute-done | bytes 1277984 | tf_op jit(solution)/shard_map/ppermute | solution.py:82
  349.4 1.5 collective-permute-start.17
  351.0 10.0 %collective-permute-done.25 = bf16[4,48,1536]{2,1,0:T(8,128)(2,1)S(1)} collective-permute-done((bf16[4,48,1536]{2,1,0:T(8,128)(2,1)S(1)}, bf16[4,48,1536]{2,1,0:T(8,128)(2,1)S(1)}, u32[]{:S(2)}, u32[]{:S(2)}) %collective-permute-start.25) | collective-permute-done | bytes 589856 | tf_op jit(solution)/shard_map/ppermute | solution.py:82
  361.2 1.5 collective-permute-start.26
  363.7 2.4 collective-permute-start.28
  366.4 3.6 collective-permute-done.26
  369.9 5.7 %collective-permute-start.34 = (bf16[96,768]{1,0:T(8,128)(2,1)S(1)}, bf16[96,768]{1,0:T(8,128)(2,1)S(1)}, u32[]{:S(2)}, u32[]{:S(2)}) collective-permute-start(bf16[96,768]{1,0:T(8,128)(2,1)S(1)} %get-tuple-element.188), channel_id=1, source_target_pairs={{0,16},{1,17},{2,18},{3,19},{4,20},{5,21},{6,22},{7,23},{8,24},{9,... | collective-permute-start | bytes 442376 | tf_op jit(solution)/shard_map/ppermute | solution.py:82
  375.7 3.8 collective-permute-done.27
  379.5 5.5 %collective-permute-start.35 = (bf16[96,768]{1,0:T(8,128)(2,1)S(1)}, bf16[96,768]{1,0:T(8,128)(2,1)S(1)}, u32[]{:S(2)}, u32[]{:S(2)}) collective-permute-start(bf16[96,768]{1,0:T(8,128)(2,1)S(1)} %get-tuple-element.187), channel_id=1, source_target_pairs={{0,24},{1,25},{2,26},{3,27},{4,28},{5,29},{6,30},{7,31},{8,0},{9,1... | collective-permute-start | bytes 442376 | tf_op jit(solution)/shard_map/ppermute | solution.py:82
  385.2 2.1 collective-permute-done.34
  389.5 2.6 collective-permute-start.18
  392.1 1.5 collective-permute-start.19
  395.2 3.0 collective-permute-done.18
  398.3 5.3 %collective-permute-done.19 = bf16[208,384]{1,0:T(8,128)(2,1)S(1)} collective-permute-done((bf16[208,384]{1,0:T(8,128)(2,1)S(1)}, bf16[208,384]{1,0:T(8,128)(2,1)S(1)}, u32[]{:S(2)}, u32[]{:S(2)}) %collective-permute-start.19) | collective-permute-done | bytes 159776 | tf_op jit(solution)/shard_map/ppermute | solution.py:82
  410.1 1.2 collective-permute-start.36
  412.0 2.8 collective-permute-start.37
  416.2 2.8 collective-permute-start.38
  420.4 5.2 %collective-permute-start.39 = (f32[]{:T(128)}, f32[]{:T(128)}, u32[]{:S(2)}, u32[]{:S(2)}) collective-permute-start(f32[]{:T(128)} %add.765), channel_id=1, source_target_pairs={{0,8},{1,9},{2,10},{3,11},{4,12},{5,13},{6,14},{7,15},{8,16},{9,17... | collective-permute-start | bytes 20 | tf_op jit(solution)/shard_map/ppermute | solution.py:82
  425.6 3.4 collective-permute-start.40
  429.0 1.6 collective-permute-start.41
  439.7 1.2 multiply_add_fusion
  (287 shorter events, 40.2 us)
Async XLA Ops:
  7.3 104.3 %all-gather.3.cloned.1.call-start = ((), (), s32[]{:S(2)}) async-start(), calls=%async_computation | async-start | bytes 9732096 | tf_op jit(solution)/shard_map/all_gather | solution.py:651
  8.4 1.5 collective-permute-start.14
  10.8 6.0 %collective-permute-start = (bf16[3,48,192]{2,1,0:T(8,128)(2,1)S(1)}, bf16[3,48,192]{2,1,0:T(8,128)(2,1)S(1)}, u32[]{:S(2)}, u32[]{:S(2)}) collective-permute-start(bf16[3,48,192]{2,1,0:T(8,128)(2,1)S(1)} %constant_dynamic-slice_fusion.16), channel_id=1, source_target_pairs={{0,1},{1,0},{2,3},{3,2},{4,5},{5,4},{6,7},{7,6},{8,9},{9,8},{10,11... | collective-permute-start | bytes 165896 | tf_op jit(solution)/shard_map/ppermute | solution.py:82
  11.2 5.6 %collective-permute-start.1 = (bf16[24,384]{1,0:T(8,128)(2,1)S(1)}, bf16[24,384]{1,0:T(8,128)(2,1)S(1)}, u32[]{:S(2)}, u32[]{:S(2)}) collective-permute-start(bf16[24,384]{1,0:T(8,128)(2,1)S(1)} %constant_dynamic-slice_fusion.15), channel_id=1, source_target_pairs={{0,1},{1,0},{2,3},{3,2},{4,5},{5,4},{6,7},{7,6},{8,9},{9,8},{10,11... | collective-permute-start | bytes 55304 | tf_op jit(solution)/shard_map/ppermute | solution.py:82
  17.0 9.9 %collective-permute-start.2 = (bf16[208,384]{1,0:T(8,128)(2,1)S(1)}, bf16[208,384]{1,0:T(8,128)(2,1)S(1)}, u32[]{:S(2)}, u32[]{:S(2)}) collective-permute-start(bf16[208,384]{1,0:T(8,128)(2,1)S(1)} %get-tuple-element.208), channel_id=1, source_target_pairs={{0,8},{1,9},{2,10},{3,11},{4,12},{5,13},{6,14},{7,15},{8,16},{9,17... | collective-permute-start | bytes 479240 | tf_op jit(solution)/shard_map/ppermute | solution.py:82
  19.8 18.0 %collective-permute-start.3 = (bf16[208,384]{1,0:T(8,128)(2,1)S(1)}, bf16[208,384]{1,0:T(8,128)(2,1)S(1)}, u32[]{:S(2)}, u32[]{:S(2)}) collective-permute-start(bf16[208,384]{1,0:T(8,128)(2,1)S(1)} %get-tuple-element.208), channel_id=1, source_target_pairs={{0,16},{1,17},{2,18},{3,19},{4,20},{5,21},{6,22},{7,23},{8,24},{9,... | collective-permute-start | bytes 479240 | tf_op jit(solution)/shard_map/ppermute | solution.py:82
  22.4 15.5 %collective-permute-start.4 = (bf16[208,384]{1,0:T(8,128)(2,1)S(1)}, bf16[208,384]{1,0:T(8,128)(2,1)S(1)}, u32[]{:S(2)}, u32[]{:S(2)}) collective-permute-start(bf16[208,384]{1,0:T(8,128)(2,1)S(1)} %get-tuple-element.208), channel_id=1, source_target_pairs={{0,24},{1,25},{2,26},{3,27},{4,28},{5,29},{6,30},{7,31},{8,0},{9,1... | collective-permute-start | bytes 479240 | tf_op jit(solution)/shard_map/ppermute | solution.py:82
  38.0 38.8 %copy-start.6 = (bf16[4,208,384]{2,1,0:T(8,128)(2,1)}, bf16[4,208,384]{2,1,0:T(8,128)(2,1)S(1)}, u32[]{:S(2)}) copy-start(bf16[4,208,384]{2,1,0:T(8,128)(2,1)S(1)} %pad_maximum_fusion.rest_0_) | copy-start | bytes 1916932
  38.0 20.5 %collective-permute-start.6 = (bf16[4,208,384]{2,1,0:T(8,128)(2,1)S(1)}, bf16[4,208,384]{2,1,0:T(8,128)(2,1)S(1)}, u32[]{:S(2)}, u32[]{:S(2)}) collective-permute-start(bf16[4,208,384]{2,1,0:T(8,128)(2,1)S(1)} %pad_maximum_fusion.rest_0_), channel_id=1, source_target_pairs={{0,4},{1,5},{2,6},{3,7},{4,0},{5,1},{6,2},{7,3},{8,12},{9,13},{10,... | collective-permute-start | bytes 1916936 | tf_op jit(solution)/shard_map/ppermute | solution.py:82
  39.7 24.2 %collective-permute-start.5 = (bf16[4,208,384]{2,1,0:T(8,128)(2,1)S(1)}, bf16[4,208,384]{2,1,0:T(8,128)(2,1)S(1)}, u32[]{:S(2)}, u32[]{:S(2)}) collective-permute-start(bf16[4,208,384]{2,1,0:T(8,128)(2,1)S(1)} %pad_maximum_fusion.rest_0_), channel_id=1, source_target_pairs={{0,2},{1,3},{2,0},{3,1},{4,6},{5,7},{6,4},{7,5},{8,10},{9,11},{10,... | collective-permute-start | bytes 1916936 | tf_op jit(solution)/shard_map/ppermute | solution.py:82
  41.2 23.5 %collective-permute-start.9 = (bf16[4,208,384]{2,1,0:T(8,128)(2,1)S(1)}, bf16[4,208,384]{2,1,0:T(8,128)(2,1)S(1)}, u32[]{:S(2)}, u32[]{:S(2)}) collective-permute-start(bf16[4,208,384]{2,1,0:T(8,128)(2,1)S(1)} %pad_maximum_fusion.rest_0_), channel_id=1, source_target_pairs={{0,1},{1,0},{2,3},{3,2},{4,5},{5,4},{6,7},{7,6},{8,9},{9,8},{10,11... | collective-permute-start | bytes 1916936 | tf_op jit(solution)/shard_map/ppermute | solution.py:82
  58.5 18.3 %copy-start.7 = (bf16[4,208,384]{2,1,0:T(8,128)(2,1)}, bf16[4,208,384]{2,1,0:T(8,128)(2,1)S(1)}, u32[]{:S(2)}) copy-start(bf16[4,208,384]{2,1,0:T(8,128)(2,1)S(1)} %collective-permute-done.6.rest_2_) | copy-start | bytes 1916932
  58.5 12.3 %collective-permute-start.8 = (bf16[2,208,384]{2,1,0:T(8,128)(2,1)S(1)}, bf16[2,208,384]{2,1,0:T(8,128)(2,1)S(1)}, u32[]{:S(2)}, u32[]{:S(2)}) collective-permute-start(bf16[2,208,384]{2,1,0:T(8,128)(2,1)S(1)} %slice.237), channel_id=1, source_target_pairs={{0,2},{1,3},{2,0},{3,1},{4,6},{5,7},{6,4},{7,5},{8,10},{9,11},{10,... | collective-permute-start | bytes 958472 | tf_op jit(solution)/shard_map/ppermute | solution.py:82
  64.0 12.8 %copy-start.8 = (bf16[4,208,384]{2,1,0:T(8,128)(2,1)}, bf16[4,208,384]{2,1,0:T(8,128)(2,1)S(1)}, u32[]{:S(2)}) copy-start(bf16[4,208,384]{2,1,0:T(8,128)(2,1)S(1)} %collective-permute-done.5.rest_1_) | copy-start | bytes 1916932
  64.0 7.1 %collective-permute-start.7 = (bf16[2,208,384]{2,1,0:T(8,128)(2,1)S(1)}, bf16[2,208,384]{2,1,0:T(8,128)(2,1)S(1)}, u32[]{:S(2)}, u32[]{:S(2)}) collective-permute-start(bf16[2,208,384]{2,1,0:T(8,128)(2,1)S(1)} %slice.234), channel_id=1, source_target_pairs={{0,4},{1,5},{2,6},{3,7},{4,0},{5,1},{6,2},{7,3},{8,12},{9,13},{10,... | collective-permute-start | bytes 958472 | tf_op jit(solution)/shard_map/ppermute | solution.py:82
  64.1 8.8 %collective-permute-start.11 = (bf16[4,208,384]{2,1,0:T(8,128)(2,1)S(1)}, bf16[4,208,384]{2,1,0:T(8,128)(2,1)S(1)}, u32[]{:S(2)}, u32[]{:S(2)}) collective-permute-start(bf16[4,208,384]{2,1,0:T(8,128)(2,1)S(1)} %collective-permute-done.6.rest_2_), channel_id=1, source_target_pairs={{0,1},{1,0},{2,3},{3,2},{4,5},{5,4},{6,7},{7,6},{8,9},{9,8},{10,11... | collective-permute-start | bytes 1916936 | tf_op jit(solution)/shard_map/ppermute | solution.py:82
  64.2 8.8 %collective-permute-start.10 = (bf16[4,208,384]{2,1,0:T(8,128)(2,1)S(1)}, bf16[4,208,384]{2,1,0:T(8,128)(2,1)S(1)}, u32[]{:S(2)}, u32[]{:S(2)}) collective-permute-start(bf16[4,208,384]{2,1,0:T(8,128)(2,1)S(1)} %collective-permute-done.5.rest_1_), channel_id=1, source_target_pairs={{0,1},{1,0},{2,3},{3,2},{4,5},{5,4},{6,7},{7,6},{8,9},{9,8},{10,11... | collective-permute-start | bytes 1916936 | tf_op jit(solution)/shard_map/ppermute | solution.py:82
  64.7 12.1 %copy-start.13 = (bf16[4,208,384]{2,1,0:T(8,128)(2,1)}, bf16[4,208,384]{2,1,0:T(8,128)(2,1)S(1)}, u32[]{:S(2)}) copy-start(bf16[4,208,384]{2,1,0:T(8,128)(2,1)S(1)} %collective-permute-done.9.rest_5_) | copy-start | bytes 1916932
  70.8 1.6 collective-permute-start.13
  71.1 1.8 collective-permute-start.12
  185.4 103.4 %collective-permute-start.30 = (bf16[4,2,2,96,768]{4,3,0,1,2:T(8,128)(2,1)}, bf16[4,2,2,96,768]{4,3,0,1,2:T(8,128)(2,1)}, u32[]{:S(2)}, u32[]{:S(2)}) collective-permute-start(bf16[4,2,2,96,768]{4,3,0,1,2:T(8,128)(2,1)} %bitcast.230), channel_id=1, source_target_pairs={{0,1},{1,0},{2,3},{3,2},{4,5},{5,4},{6,7},{7,6},{8,9},{9,8},{10,11... | collective-permute-start | bytes 7077896 | tf_op jit(solution)/shard_map/ppermute | solution.py:82
  222.3 59.9 %collective-permute-start.23 = (bf16[4,2,2,48,1536]{4,3,0,2,1:T(8,128)(2,1)}, bf16[4,2,2,48,1536]{4,3,0,2,1:T(8,128)(2,1)}, u32[]{:S(2)}, u32[]{:S(2)}) collective-permute-start(bf16[4,2,2,48,1536]{4,3,0,2,1:T(8,128)(2,1)} %bitcast.231), channel_id=1, source_target_pairs={{0,1},{1,0},{2,3},{3,2},{4,5},{5,4},{6,7},{7,6},{8,9},{9,8},{10,11... | collective-permute-start | bytes 7077896 | tf_op jit(solution)/shard_map/ppermute | solution.py:82
  270.0 4.8 %copy-start.35 = (f32[8,768]{1,0:T(8,128)S(1)}, f32[8,768]{1,0:T(8,128)}, u32[]{:S(2)}) copy-start(f32[8,768]{1,0:T(8,128)} %get-tuple-element.58) | copy-start | bytes 73732
  270.0 4.9 %copy-start.36 = (bf16[7680]{0:T(1024)(128)(2,1)S(1)}, bf16[7680]{0:T(1024)(128)(2,1)}, u32[]{:S(2)}) copy-start(bf16[7680]{0:T(1024)(128)(2,1)} %custom-call) | copy-start | bytes 46084
  270.0 5.1 %copy-start.38 = (f32[1,3072]{1,0:T(1,128)S(1)}, f32[1,3072]{1,0:T(1,128)}, u32[]{:S(2)}) copy-start(f32[1,3072]{1,0:T(1,128)} %get-tuple-element.59) | copy-start | bytes 36868
  270.0 6.6 %copy-start.39 = (f32[2,768]{1,0:T(2,128)S(1)}, f32[2,768]{1,0:T(2,128)}, u32[]{:S(2)}) copy-start(f32[2,768]{1,0:T(2,128)} %get-tuple-element.60) | copy-start | bytes 18436
  280.7 13.3 %collective-permute-start.15 = (bf16[4,2,2,208,384]{4,3,0,1,2:T(8,128)(2,1)}, bf16[4,2,2,208,384]{4,3,0,1,2:T(8,128)(2,1)}, u32[]{:S(2)}, u32[]{:S(2)}) collective-permute-start(bf16[4,2,2,208,384]{4,3,0,1,2:T(8,128)(2,1)} %fusion.5), channel_id=1, source_target_pairs={{0,1},{1,0},{2,3},{3,2},{4,5},{5,4},{6,7},{7,6},{8,9},{9,8},{10,11... | collective-permute-start | bytes 7667720 | tf_op jit(solution)/shard_map/ppermute | solution.py:82
  286.1 5.3 %copy-start.3 = (bf16[4,2,2,48,1536]{4,3,0,2,1:T(8,128)(2,1)}, bf16[4,2,2,48,1536]{4,3,0,2,1:T(8,128)(2,1)S(1)}, u32[]{:S(2)}) copy-start(bf16[4,2,2,48,1536]{4,3,0,2,1:T(8,128)(2,1)S(1)} %fusion.3) | copy-start | bytes 7077892
  287.4 28.5 %collective-permute-start.24 = (bf16[4,2,48,1536]{3,2,0,1:T(8,128)(2,1)}, bf16[4,2,48,1536]{3,2,0,1:T(8,128)(2,1)}, u32[]{:S(2)}, u32[]{:S(2)}) collective-permute-start(bf16[4,2,48,1536]{3,2,0,1:T(8,128)(2,1)} %dynamic-slice_bitcast_fusion.2), channel_id=1, source_target_pairs={{0,4},{1,5},{2,6},{3,7},{4,0},{5,1},{6,2},{7,3},{8,12},{9,13},{10,... | collective-permute-start | bytes 3538952 | tf_op jit(solution)/shard_map/ppermute | solution.py:82
  292.6 29.1 %collective-permute-start.31 = (bf16[4,2,96,768]{3,2,0,1:T(8,128)(2,1)}, bf16[4,2,96,768]{3,2,0,1:T(8,128)(2,1)}, u32[]{:S(2)}, u32[]{:S(2)}) collective-permute-start(bf16[4,2,96,768]{3,2,0,1:T(8,128)(2,1)} %dynamic-slice_bitcast_fusion.1), channel_id=1, source_target_pairs={{0,2},{1,3},{2,0},{3,1},{4,6},{5,7},{6,4},{7,5},{8,10},{9,11},{10,... | collective-permute-start | bytes 3538952 | tf_op jit(solution)/shard_map/ppermute | solution.py:82
  297.3 51.7 %collective-permute-start.16 = (bf16[4,2,208,384]{3,2,0,1:T(8,128)(2,1)}, bf16[4,2,208,384]{3,2,0,1:T(8,128)(2,1)S(1)}, u32[]{:S(2)}, u32[]{:S(2)}) collective-permute-start(bf16[4,2,208,384]{3,2,0,1:T(8,128)(2,1)} %dynamic-slice_bitcast_fusion), channel_id=1, source_target_pairs={{0,2},{1,3},{2,0},{3,1},{4,6},{5,7},{6,4},{7,5},{8,10},{9,11},{10,... | collective-permute-start | bytes 3833864 | tf_op jit(solution)/shard_map/ppermute | solution.py:82
  317.8 43.2 %collective-permute-start.25 = (bf16[4,48,1536]{2,1,0:T(8,128)(2,1)S(1)}, bf16[4,48,1536]{2,1,0:T(8,128)(2,1)S(1)}, u32[]{:S(2)}, u32[]{:S(2)}) collective-permute-start(bf16[4,48,1536]{2,1,0:T(8,128)(2,1)S(1)} %dynamic-slice_bitcast_fusion.5), channel_id=1, source_target_pairs={{0,2},{1,3},{2,0},{3,1},{4,6},{5,7},{6,4},{7,5},{8,10},{9,11},{10,... | collective-permute-start | bytes 1769480 | tf_op jit(solution)/shard_map/ppermute | solution.py:82
  323.3 42.7 %collective-permute-start.32 = (bf16[4,96,768]{2,1,0:T(8,128)(2,1)S(1)}, bf16[4,96,768]{2,1,0:T(8,128)(2,1)S(1)}, u32[]{:S(2)}, u32[]{:S(2)}) collective-permute-start(bf16[4,96,768]{2,1,0:T(8,128)(2,1)S(1)} %dynamic-slice_bitcast_fusion.4), channel_id=1, source_target_pairs={{0,4},{1,5},{2,6},{3,7},{4,0},{5,1},{6,2},{7,3},{8,12},{9,13},{10,... | collective-permute-start | bytes 1769480 | tf_op jit(solution)/shard_map/ppermute | solution.py:82
  349.4 39.7 %collective-permute-start.17 = (bf16[4,208,384]{2,1,0:T(8,128)(2,1)S(1)}, bf16[4,208,384]{2,1,0:T(8,128)(2,1)S(1)}, u32[]{:S(2)}, u32[]{:S(2)}) collective-permute-start(bf16[4,208,384]{2,1,0:T(8,128)(2,1)S(1)} %dynamic-slice_bitcast_fusion.3), channel_id=1, source_target_pairs={{0,4},{1,5},{2,6},{3,7},{4,0},{5,1},{6,2},{7,3},{8,12},{9,13},{10,... | collective-permute-start | bytes 1916936 | tf_op jit(solution)/shard_map/ppermute | solution.py:82
  361.2 8.7 %collective-permute-start.26 = (bf16[48,1536]{1,0:T(8,128)(2,1)S(1)}, bf16[48,1536]{1,0:T(8,128)(2,1)S(1)}, u32[]{:S(2)}, u32[]{:S(2)}) collective-permute-start(bf16[48,1536]{1,0:T(8,128)(2,1)S(1)} %get-tuple-element.189), channel_id=1, source_target_pairs={{0,8},{1,9},{2,10},{3,11},{4,12},{5,13},{6,14},{7,15},{8,16},{9,17... | collective-permute-start | bytes 442376 | tf_op jit(solution)/shard_map/ppermute | solution.py:82
  362.7 16.8 %collective-permute-start.27 = (bf16[48,1536]{1,0:T(8,128)(2,1)S(1)}, bf16[48,1536]{1,0:T(8,128)(2,1)S(1)}, u32[]{:S(2)}, u32[]{:S(2)}) collective-permute-start(bf16[48,1536]{1,0:T(8,128)(2,1)S(1)} %get-tuple-element.191), channel_id=1, source_target_pairs={{0,16},{1,17},{2,18},{3,19},{4,20},{5,21},{6,22},{7,23},{8,24},{9,... | collective-permute-start | bytes 442376 | tf_op jit(solution)/shard_map/ppermute | solution.py:82
  363.7 21.3 %collective-permute-start.28 = (bf16[48,1536]{1,0:T(8,128)(2,1)S(1)}, bf16[48,1536]{1,0:T(8,128)(2,1)S(1)}, u32[]{:S(2)}, u32[]{:S(2)}) collective-permute-start(bf16[48,1536]{1,0:T(8,128)(2,1)S(1)} %get-tuple-element.190), channel_id=1, source_target_pairs={{0,24},{1,25},{2,26},{3,27},{4,28},{5,29},{6,30},{7,31},{8,0},{9,1... | collective-permute-start | bytes 442376 | tf_op jit(solution)/shard_map/ppermute | solution.py:82
  366.3 18.9 %collective-permute-start.33 = (bf16[96,768]{1,0:T(8,128)(2,1)S(1)}, bf16[96,768]{1,0:T(8,128)(2,1)S(1)}, u32[]{:S(2)}, u32[]{:S(2)}) collective-permute-start(bf16[96,768]{1,0:T(8,128)(2,1)S(1)} %get-tuple-element.186), channel_id=1, source_target_pairs={{0,8},{1,9},{2,10},{3,11},{4,12},{5,13},{6,14},{7,15},{8,16},{9,17... | collective-permute-start | bytes 442376 | tf_op jit(solution)/shard_map/ppermute | solution.py:82
  369.9 17.4 %collective-permute-start.34 = (bf16[96,768]{1,0:T(8,128)(2,1)S(1)}, bf16[96,768]{1,0:T(8,128)(2,1)S(1)}, u32[]{:S(2)}, u32[]{:S(2)}) collective-permute-start(bf16[96,768]{1,0:T(8,128)(2,1)S(1)} %get-tuple-element.188), channel_id=1, source_target_pairs={{0,16},{1,17},{2,18},{3,19},{4,20},{5,21},{6,22},{7,23},{8,24},{9,... | collective-permute-start | bytes 442376 | tf_op jit(solution)/shard_map/ppermute | solution.py:82
  379.5 9.0 %collective-permute-start.35 = (bf16[96,768]{1,0:T(8,128)(2,1)S(1)}, bf16[96,768]{1,0:T(8,128)(2,1)S(1)}, u32[]{:S(2)}, u32[]{:S(2)}) collective-permute-start(bf16[96,768]{1,0:T(8,128)(2,1)S(1)} %get-tuple-element.187), channel_id=1, source_target_pairs={{0,24},{1,25},{2,26},{3,27},{4,28},{5,29},{6,30},{7,31},{8,0},{9,1... | collective-permute-start | bytes 442376 | tf_op jit(solution)/shard_map/ppermute | solution.py:82
  385.1 9.4 %collective-permute-start.29 = (f32[24,1536]{1,0:T(8,128)S(1)}, f32[24,1536]{1,0:T(8,128)S(1)}, u32[]{:S(2)}, u32[]{:S(2)}) collective-permute-start(f32[24,1536]{1,0:T(8,128)S(1)} %constant_dynamic-slice_fusion.2), channel_id=1, source_target_pairs={{0,1},{1,0},{2,3},{3,2},{4,5},{5,4},{6,7},{7,6},{8,9},{9,8},{10,11... | collective-permute-start | bytes 442376 | tf_op jit(solution)/shard_map/ppermute | solution.py:82
  389.3 44.1 %copy-start.40 = (f32[2,3,8]{2,0,1:T(2,128)S(1)}, f32[2,3,8]{2,0,1:T(2,128)}, u32[]{:S(2)}) copy-start(f32[2,3,8]{2,0,1:T(2,128)} %param.39) | copy-start | bytes 580
  389.3 44.1 %copy-start.41 = (f32[2,3,8]{2,0,1:T(2,128)S(1)}, f32[2,3,8]{2,0,1:T(2,128)}, u32[]{:S(2)}) copy-start(f32[2,3,8]{2,0,1:T(2,128)} %param.37) | copy-start | bytes 580
  389.4 44.0 %copy-start.42 = (f32[2,3,8]{2,0,1:T(2,128)S(1)}, f32[2,3,8]{2,0,1:T(2,128)}, u32[]{:S(2)}) copy-start(f32[2,3,8]{2,0,1:T(2,128)} %param.38) | copy-start | bytes 580
  389.4 46.4 %copy-start.9 = (f32[24,3072]{1,0:T(8,128)S(1)}, f32[24,3072]{1,0:T(8,128)}, u32[]{:S(2)}) copy-start(f32[24,3072]{1,0:T(8,128)} %param.44) | copy-start | bytes 884740
  389.4 46.4 %copy-start.22 = (f32[24,3072]{1,0:T(8,128)S(1)}, f32[24,3072]{1,0:T(8,128)}, u32[]{:S(2)}) copy-start(f32[24,3072]{1,0:T(8,128)} %param.47) | copy-start | bytes 884740
  389.4 46.4 %copy-start.23 = (f32[24,3072]{1,0:T(8,128)S(1)}, f32[24,3072]{1,0:T(8,128)}, u32[]{:S(2)}) copy-start(f32[24,3072]{1,0:T(8,128)} %param.45) | copy-start | bytes 884740
  389.4 46.4 %copy-start.24 = (f32[24,3072]{1,0:T(8,128)S(1)}, f32[24,3072]{1,0:T(8,128)}, u32[]{:S(2)}) copy-start(f32[24,3072]{1,0:T(8,128)} %param.46) | copy-start | bytes 884740
  389.5 8.8 %collective-permute-start.18 = (bf16[208,384]{1,0:T(8,128)(2,1)S(1)}, bf16[208,384]{1,0:T(8,128)(2,1)S(1)}, u32[]{:S(2)}, u32[]{:S(2)}) collective-permute-start(bf16[208,384]{1,0:T(8,128)(2,1)S(1)} %get-tuple-element.163), channel_id=1, source_target_pairs={{0,8},{1,9},{2,10},{3,11},{4,12},{5,13},{6,14},{7,15},{8,16},{9,17... | collective-permute-start | bytes 479240 | tf_op jit(solution)/shard_map/ppermute | solution.py:82
  392.1 11.5 %collective-permute-start.19 = (bf16[208,384]{1,0:T(8,128)(2,1)S(1)}, bf16[208,384]{1,0:T(8,128)(2,1)S(1)}, u32[]{:S(2)}, u32[]{:S(2)}) collective-permute-start(bf16[208,384]{1,0:T(8,128)(2,1)S(1)} %get-tuple-element.165), channel_id=1, source_target_pairs={{0,16},{1,17},{2,18},{3,19},{4,20},{5,21},{6,22},{7,23},{8,24},{9,... | collective-permute-start | bytes 479240 | tf_op jit(solution)/shard_map/ppermute | solution.py:82
  393.6 10.0 %collective-permute-start.20 = (bf16[208,384]{1,0:T(8,128)(2,1)S(1)}, bf16[208,384]{1,0:T(8,128)(2,1)S(1)}, u32[]{:S(2)}, u32[]{:S(2)}) collective-permute-start(bf16[208,384]{1,0:T(8,128)(2,1)S(1)} %get-tuple-element.164), channel_id=1, source_target_pairs={{0,24},{1,25},{2,26},{3,27},{4,28},{5,29},{6,30},{7,31},{8,0},{9,1... | collective-permute-start | bytes 479240 | tf_op jit(solution)/shard_map/ppermute | solution.py:82
  403.7 33.4 %copy-start.21 = (f32[24,768]{1,0:T(8,128)S(1)}, f32[24,768]{1,0:T(8,128)}, u32[]{:S(2)}) copy-start(f32[24,768]{1,0:T(8,128)} %param.40) | copy-start | bytes 221188
  403.7 33.4 %copy-start.32 = (f32[24,768]{1,0:T(8,128)S(1)}, f32[24,768]{1,0:T(8,128)}, u32[]{:S(2)}) copy-start(f32[24,768]{1,0:T(8,128)} %param.43) | copy-start | bytes 221188
  403.7 1.3 collective-permute-start.22
  403.8 34.0 %copy-start.11 = (f32[3,96,192]{2,1,0:T(8,128)S(1)}, f32[3,96,192]{2,1,0:T(8,128)}, u32[]{:S(2)}) copy-start(f32[3,96,192]{2,1,0:T(8,128)} %param.32) | copy-start | bytes 663556
  403.8 34.0 %copy-start.25 = (f32[3,96,192]{2,1,0:T(8,128)S(1)}, f32[3,96,192]{2,1,0:T(8,128)}, u32[]{:S(2)}) copy-start(f32[3,96,192]{2,1,0:T(8,128)} %param.35) | copy-start | bytes 663556
  403.8 34.0 %copy-start.26 = (f32[3,96,192]{2,1,0:T(8,128)S(1)}, f32[3,96,192]{2,1,0:T(8,128)}, u32[]{:S(2)}) copy-start(f32[3,96,192]{2,1,0:T(8,128)} %param.33) | copy-start | bytes 663556
  404.6 1.5 collective-permute-start.21
  410.1 1.3 collective-permute-start.36
  412.0 3.6 collective-permute-start.37
  416.2 3.6 collective-permute-start.38
  420.4 10.2 %collective-permute-start.39 = (f32[]{:T(128)}, f32[]{:T(128)}, u32[]{:S(2)}, u32[]{:S(2)}) collective-permute-start(f32[]{:T(128)} %add.765), channel_id=1, source_target_pairs={{0,8},{1,9},{2,10},{3,11},{4,12},{5,13},{6,14},{7,15},{8,16},{9,17... | collective-permute-start | bytes 20 | tf_op jit(solution)/shard_map/ppermute | solution.py:82
  425.6 5.6 %collective-permute-start.40 = (f32[]{:T(128)}, f32[]{:T(128)}, u32[]{:S(2)}, u32[]{:S(2)}) collective-permute-start(f32[]{:T(128)} %add.765), channel_id=1, source_target_pairs={{0,16},{1,17},{2,18},{3,19},{4,20},{5,21},{6,22},{7,23},{8,24},{9,... | collective-permute-start | bytes 20 | tf_op jit(solution)/shard_map/ppermute | solution.py:82
  429.0 3.5 collective-permute-start.41
  (27 other events, 87.1 us)
Sparse Core Ops, SparseCore 0:
  11.6 99.9 all-gather.2
